TPU v7x, 512 devices: a whole 4x8x8 slice. The times are simulated.
512 devices in a mesh: ctx: 128 (over x_hi, y, z), exp: 4 (over x_lo, core).
Axes of the slice: x: 4 (x_hi: 2, x_lo: 2; x = x_hi * 2 + x_lo), y: 8, z: 8, core: 2. Of those that a mesh axis runs over, the one named last changes fastest.
Arguments:
- hidden_state_stream: bfloat16 [32768, 2048], P('ctx', 'exp'), may hold values from -6 to 6
- question_vectors: bfloat16 [32768, 2048], P('ctx', 'exp'), may hold values from -6 to 6
- memory_lookup_vectors: bfloat16 [64, 512, 2048], P(None, 'ctx', 'exp'), may hold values from -6 to 6
- content_vectors: bfloat16 [64, 512, 2048], P(None, 'ctx', 'exp'), may hold values from -6 to 6
- logit_multiplier: float32 [16], P('exp'), may hold values from 1 to 4
- chosen_tile_lists: int32 [64, 4], replicated, may hold values from 0 to 63, all different within a row
- premix_rmsnorm_scaling: float32 [2048], P('exp'), may hold values from 0.1 to 1.9
- routing_choice_ids: int32 [32768, 2], P('ctx'), may hold values from 0 to 63, all different within a row; in each aligned block of 256 rows (0 to 255, 256 to 511, ...) at most 12 rows name the same one
- routing_shares: float32 [32768, 2], P('ctx'), may hold values from 0.25 to 1
- gating_matrix: bfloat16 [128, 704, 2048], P('ctx', 'exp'), may hold values from -0.125 to 0.125
- raising_matrix: bfloat16 [128, 704, 2048], P('ctx', 'exp'), may hold values from -0.125 to 0.125
- lowering_matrix: bfloat16 [128, 704, 2048], P('ctx', None, 'exp'), may hold values from -0.15625 to 0.15625
Outputs:
- attended: bfloat16 [32768, 2048], P('ctx', 'exp')
- mixed: bfloat16 [32768, 2048], P('ctx', 'exp')
Inputs may be any that keep to these rules, and one draw needn't show every extreme that they name: `chosen_tile_lists`: each row names 4 different blocks. `routing_choice_ids`: each event names 2 different experts; among the 256 events of one index of ctx (aligned blocks) at most 12 name one expert.
All inputs are finite; a program needn't handle non-finite values.
Results may differ from a plain program's by a relative error of at most 0.011.
Values may be sent and summed in bfloat16 or wider, within the bound.
A program may use at most 64 MiB of HBM per device.

v0:
```python
import math

import jax
import jax.numpy as jnp
from jax import lax
from jax.sharding import PartitionSpec as P

D = 2048
EXPERTS = 64
CAP = 12


def unit_rows(tensor, width):
    shaped = tensor.astype(jnp.float32).reshape(
        tensor.shape[:-1] + (tensor.shape[-1] // width, width)
    )
    scaled = shaped * lax.rsqrt(jnp.mean(shaped * shaped, axis=-1, keepdims=True) + 1e-06)
    return scaled.reshape(tensor.shape).astype(jnp.bfloat16)


def slot_ranks(route_ids, experts):
    onehot = (route_ids[:, :, None] == jnp.arange(experts, dtype=jnp.int32)[None, None, :]).astype(
        jnp.int32
    )
    counts = jnp.sum(onehot, axis=1)
    before = jnp.cumsum(counts, axis=0) - counts
    return jnp.sum(onehot * before[:, None, :], axis=2)


def partial_attend(query_rows, key_rows, value_rows, multiplier_vector):
    scores = jnp.einsum("qhd,khd->hqk", query_rows, key_rows, preferred_element_type=jnp.float32)
    expo = jnp.exp(scores * multiplier_vector[:, None, None])
    totals = jnp.sum(expo, axis=2)
    weighted = jnp.einsum(
        "hqk,khd->qhd", expo.astype(jnp.bfloat16), value_rows, preferred_element_type=jnp.float32
    )
    return (weighted, totals)


def attend_whole(
    key_unit,
    content_vectors,
    query_unit,
    picks,
    group_rows,
    local_attention_groups,
    channel_dimension,
    multiplier_vector,
):
    send_keys = jnp.take(key_unit, picks, axis=0)
    send_values = jnp.take(content_vectors, picks, axis=0)
    got_keys, got_values = (
        lax.all_to_all(send_keys, "ctx", split_axis=0, concat_axis=0, tiled=True),
        lax.all_to_all(send_values, "ctx", split_axis=0, concat_axis=0, tiled=True),
    )
    key_rows = got_keys[:, 0].reshape(-1, local_attention_groups, channel_dimension)
    value_rows = got_values[:, 0].reshape(-1, local_attention_groups, channel_dimension)
    query_rows = query_unit.reshape(group_rows, local_attention_groups, channel_dimension)
    weighted, totals = partial_attend(query_rows, key_rows, value_rows, multiplier_vector)
    outputs = (
        (weighted / jnp.transpose(totals)[:, :, None])
        .astype(jnp.bfloat16)
        .reshape(group_rows, local_attention_groups * channel_dimension)
    )
    return outputs


def per_device(
    hidden_state_stream,
    question_vectors,
    memory_lookup_vectors,
    content_vectors,
    logit_multiplier,
    chosen_tile_lists,
    premix_rmsnorm_scaling,
    routing_choice_ids,
    routing_shares,
    gating_matrix,
    raising_matrix,
    lowering_matrix,
):
    ctx_size = lax.axis_size("ctx")
    tok_local, width_local = question_vectors.shape
    local_attention_groups = logit_multiplier.shape[0]
    channel_dimension = width_local // local_attention_groups
    block_rows = memory_lookup_vectors.shape[1] * ctx_size
    groups = max(1, tok_local // block_rows)
    group_rows = tok_local // groups
    dest_ids = jnp.arange(ctx_size, dtype=jnp.int32)
    group_ids = jnp.arange(groups, dtype=jnp.int32)
    wanted = (dest_ids[:, None] * tok_local + group_ids[None, :] * group_rows) // block_rows
    picks = jnp.take(chosen_tile_lists, wanted, axis=0)
    key_unit = unit_rows(memory_lookup_vectors, channel_dimension)
    query_unit = unit_rows(question_vectors, channel_dimension)
    multiplier_vector = logit_multiplier / math.sqrt(channel_dimension)
    attended = attend_whole(
        key_unit,
        content_vectors,
        query_unit,
        picks,
        group_rows,
        local_attention_groups,
        channel_dimension,
        multiplier_vector,
    )
    summed = hidden_state_stream.astype(jnp.float32) + attended.astype(jnp.float32)
    squares = lax.psum(jnp.sum(summed * summed, axis=1), "exp")
    normed = (
        summed * lax.rsqrt(squares / D + 1e-05)[:, None] * premix_rmsnorm_scaling[None, :]
    ).astype(jnp.bfloat16)
    pieces_local = gating_matrix.shape[0]
    split_count = pieces_local * ctx_size // EXPERTS
    capacity = CAP
    ranks = slot_ranks(routing_choice_ids, EXPERTS)
    offsets = jnp.arange(split_count, dtype=jnp.int32) * capacity
    targets = (routing_choice_ids * (split_count * capacity) + ranks)[:, :, None] + offsets[
        None, None, :
    ]
    slots_all = pieces_local * ctx_size * capacity
    dispatch_table = jnp.any(
        jnp.arange(slots_all, dtype=jnp.int32)[:, None, None, None] == targets[None], axis=(2, 3)
    ).astype(jnp.bfloat16)
    outgoing = jnp.dot(dispatch_table, normed, preferred_element_type=jnp.float32).astype(
        jnp.bfloat16
    )
    outgoing = outgoing.reshape(ctx_size, pieces_local, capacity, width_local)
    arrived = lax.all_to_all(
        lax.all_to_all(outgoing, "ctx", split_axis=0, concat_axis=0, tiled=True),
        "exp",
        split_axis=2,
        concat_axis=3,
        tiled=True,
    )
    full_gate, full_up, full_down = (
        lax.all_gather(gating_matrix, "exp", axis=1, tiled=True),
        lax.all_gather(raising_matrix, "exp", axis=1, tiled=True),
        lax.all_gather(lowering_matrix, "exp", axis=2, tiled=True),
    )
    gate_out = jnp.einsum("nplf,phf->nplh", arrived, full_gate, preferred_element_type=jnp.float32)
    up_out = jnp.einsum("nplf,phf->nplh", arrived, full_up, preferred_element_type=jnp.float32)
    activated = (jax.nn.silu(gate_out) * up_out).astype(jnp.bfloat16)
    produced = jnp.einsum(
        "nplh,phf->nplf", activated, full_down, preferred_element_type=jnp.float32
    ).astype(jnp.bfloat16)
    returned = lax.all_to_all(
        lax.all_to_all(produced, "ctx", split_axis=0, concat_axis=0, tiled=True),
        "exp",
        split_axis=3,
        concat_axis=2,
        tiled=True,
    )
    flat_back = returned.reshape(slots_all, width_local)
    picked = jnp.take(flat_back, targets.reshape(-1), axis=0).reshape(
        tok_local, 2, split_count, width_local
    )
    expert_sum = jnp.einsum("tksf,tk->tf", picked.astype(jnp.float32), routing_shares)
    mixed = (summed + expert_sum).astype(jnp.bfloat16)
    return (attended, mixed)


def solution(mesh):
    in_specs = (
        P("ctx", "exp"),
        P("ctx", "exp"),
        P(None, "ctx", "exp"),
        P(None, "ctx", "exp"),
        P("exp"),
        P(),
        P("exp"),
        P("ctx", None),
        P("ctx", None),
        P("ctx", "exp", None),
        P("ctx", "exp", None),
        P("ctx", None, "exp"),
    )
    out_specs = (P("ctx", "exp"), P("ctx", "exp"))
    return jax.shard_map(
        per_device, mesh=mesh, in_specs=in_specs, out_specs=out_specs, check_vma=False
    )
```

profile of v0, /device:TPU:1, one launch (start us, length us, event | category | flops | bytes accessed | tf_op | source)
XLA Modules:
  0.0 407.3 jit_solution(13912037516437550237)
XLA Ops:
  8.9 1.1 convert_multiply_fusion.1
  11.8 3.0 gather_fusion.3
  14.8 3.8 gather_fusion.2
  18.7 4.8 %broadcast_select_fusion.1 = (bf16[128,1,4,4,512]{4,3,2,1,0:T(4,128)(2,1)}, bf16[128,1,4,4,512]{4,3,2,1,0:T(4,128)(2,1)}) fusion(bf16[128,1,4,4,512]{4,3,2,1,0:T(4,128)(2,1)} %bitcast.140, pred[128,4]{1,0:T(8,128)(4,1)S(1)} %get-tuple-element.15, bf16[128,1,4,4,512]{4,3,2,1,0:T(4,128)(2,1)S(1)} %bitcast.139), kind=kLoop, calls=%fused_computation.25 | loop fusion | flops 2097152 | bytes 8389120 | tf_op jit(solution)/shard_map/jit(_take)/select_n | solution.py:51
  23.4 20.8 %all-to-all-start.1 = ((bf16[128,1,4,4,512]{4,3,2,1,0:T(4,128)(2,1)}), bf16[128,1,4,4,512]{4,3,2,1,0:T(4,128)(2,1)S(1)}, u32[]{:S(2)}, u32[]{:S(2)}) async-start(bf16[128,1,4,4,512]{4,3,2,1,0:T(4,128)(2,1)} %get-tuple-element.18), calls=%async_computation.1 | async-start | bytes 4194304 | tf_op jit(solution)/shard_map/all_to_all | solution.py:53
  45.0 52.2 %all-to-all-done.1 = bf16[128,1,4,4,512]{4,3,2,1,0:T(4,128)(2,1)S(1)} async-done(((bf16[128,1,4,4,512]{4,3,2,1,0:T(4,128)(2,1)}), bf16[128,1,4,4,512]{4,3,2,1,0:T(4,128)(2,1)S(1)}, u32[]{:S(2)}, u32[]{:S(2)}) %all-to-all-start.1) | async-done | bytes 2097184 | tf_op jit(solution)/shard_map/all_to_all | solution.py:53
  97.2 11.2 %all-to-all-start = ((bf16[128,1,4,4,512]{4,3,2,1,0:T(4,128)(2,1)}), bf16[128,1,4,4,512]{4,3,2,1,0:T(4,128)(2,1)}, u32[]{:S(2)}, u32[]{:S(2)}) async-start(bf16[128,1,4,4,512]{4,3,2,1,0:T(4,128)(2,1)} %get-tuple-element.17), calls=%async_computation | async-start | bytes 4194304 | tf_op jit(solution)/shard_map/all_to_all | solution.py:54
  111.0 1.8 fusion.2
  112.8 2.2 reshape_squeeze.7
  115.0 44.8 %all-to-all-done = bf16[128,1,4,4,512]{4,3,2,1,0:T(4,128)(2,1)} async-done(((bf16[128,1,4,4,512]{4,3,2,1,0:T(4,128)(2,1)}), bf16[128,1,4,4,512]{4,3,2,1,0:T(4,128)(2,1)}, u32[]{:S(2)}, u32[]{:S(2)}) %all-to-all-start) | async-done | bytes 2097184 | tf_op jit(solution)/shard_map/all_to_all | solution.py:54
  159.9 2.7 reshape_squeeze.6
  163.0 3.4 fusion
  166.4 1.6 fusion.46
  168.3 9.2 %psum.7 = f32[256]{0:T(256)S(1)} all-reduce(f32[256]{0:T(256)S(1)} %multiply_reduce_fusion), channel_id=1, replica_groups=mesh['ctx'=128,'exp'=4] {'exp'}, use_global_device_ids=true, to_apply=%region_9.11 | all-reduce | flops 256 | bytes 2048 | tf_op jit(solution)/shard_map/psum | solution.py:107
  178.2 1.6 reshape.270
  179.7 8.9 %all-to-all-start.2 = ((bf16[128,1,12,512]{3,2,1,0:T(8,128)(2,1)}), bf16[128,1,12,512]{3,2,1,0:T(8,128)(2,1)S(1)}, u32[]{:S(2)}, u32[]{:S(2)}) async-start(bf16[128,1,12,512]{3,2,1,0:T(8,128)(2,1)} %bitcast.136), calls=%async_computation.2 | async-start | bytes 4194304 | tf_op jit(solution)/shard_map/all_to_all | solution.py:128
  189.3 52.2 %all-to-all-done.2 = bf16[128,1,12,512]{3,2,1,0:T(8,128)(2,1)S(1)} async-done(((bf16[128,1,12,512]{3,2,1,0:T(8,128)(2,1)}), bf16[128,1,12,512]{3,2,1,0:T(8,128)(2,1)S(1)}, u32[]{:S(2)}, u32[]{:S(2)}) %all-to-all-start.2) | async-done | bytes 1572896 | tf_op jit(solution)/shard_map/all_to_all | solution.py:128
  242.4 24.4 %all_to_all.50 = bf16[128,1,12,512]{3,0,1,2:T(8,128)(2,1)S(1)} all-to-all(bf16[128,1,12,512]{3,0,1,2:T(8,128)(2,1)S(1)} %copy.101), channel_id=1, replica_groups=mesh['ctx'=128,'exp'=4] {'exp'}, dimensions={2} | all-to-all | bytes 3145728 | tf_op jit(solution)/shard_map/all_to_all | solution.py:127
  266.8 1.2 copy.102
  268.0 2.4 reshape.271
  270.4 4.9 %fusion.21 = f32[128,1,3,704]{0,3,2,1:T(8,128)} fusion(bf16[128,3,2048]{2,0,1:T(8,128)(2,1)} %reshape.271, bf16[1,704,2048]{2,1,0:T(8,128)(2,1)} %all-gather.4.cloned.1.call-done), kind=kOutput, calls=%fused_computation.27 | convolution fusion | flops 1107296256 | bytes 5537792 | tf_op jit(solution)/shard_map/nplf,phf->nplh/dot_general | solution.py:139
  275.4 6.5 %fusion.15 = bf16[128,1,3,2048]{3,0,2,1:T(8,128)(2,1)S(1)} fusion(bf16[1,704,2048]{2,1,0:T(8,128)(2,1)} %all-gather.8.cloned.1.call-done, bf16[128,3,2048]{2,0,1:T(8,128)(2,1)} %reshape.271, bf16[1,704,2048]{2,1,0:T(8,128)(2,1)} %all-gather.6.cloned.1.call-done, f32[128,1,3,704]{0,3,2,1:T(8,128)} %fusion.21), kind=kOutput, calls=%fused_computation.19 | convolution fusion | flops 2217000960 | bytes 9994240 | tf_op jit(solution)/shard_map/nplh,phf->nplf/dot_general | solution.py:142
  281.9 1.4 copy.103
  283.3 64.2 %all_to_all.51 = bf16[128,1,3,2048]{3,2,1,0:T(4,128)(2,1)S(1)} all-to-all(bf16[128,1,3,2048]{3,2,1,0:T(4,128)(2,1)S(1)} %copy.103), channel_id=1, replica_groups=mesh['ctx'=128,'exp'=4] {'ctx'}, dimensions={0} | all-to-all | bytes 3145728 | tf_op jit(solution)/shard_map/all_to_all | solution.py:146
  347.5 3.5 copy.104
  351.0 6.5 %all-to-all-start.5 = ((bf16[128,1,3,2048]{0,2,1,3:T(4,128)(2,1)}), bf16[128,1,3,2048]{0,2,1,3:T(4,128)(2,1)S(1)}, u32[]{:S(2)}, u32[]{:S(2)}) async-start(bf16[128,1,3,2048]{0,2,1,3:T(4,128)(2,1)} %copy.104), calls=%async_computation.5 | async-start | bytes 4194304 | tf_op jit(solution)/shard_map/all_to_all | solution.py:145
  359.2 23.1 %all-to-all-done.5 = bf16[128,1,3,2048]{0,2,1,3:T(4,128)(2,1)S(1)} async-done(((bf16[128,1,3,2048]{0,2,1,3:T(4,128)(2,1)}), bf16[128,1,3,2048]{0,2,1,3:T(4,128)(2,1)S(1)}, u32[]{:S(2)}, u32[]{:S(2)}) %all-to-all-start.5) | async-done | bytes 1572896 | tf_op jit(solution)/shard_map/all_to_all | solution.py:145
  382.3 4.1 copy.105
  386.3 3.9 reshape.276
  390.3 4.0 gather_fusion.1
  394.7 3.6 convert_reduce_fusion
  398.3 1.6 fusion.65
  (76 shorter events, 12.5 us)
Async XLA Ops:
  7.2 7.7 %copy-start = (bf16[64,4,512]{2,1,0:T(4,128)(2,1)S(1)}, bf16[64,4,512]{2,1,0:T(4,128)(2,1)}, u32[]{:S(2)}) copy-start(bf16[64,4,512]{2,1,0:T(4,128)(2,1)} %param.17) | copy-start | bytes 786436
  8.9 2.8 copy-start.4
  23.4 73.8 %all-to-all-start.1 = ((bf16[128,1,4,4,512]{4,3,2,1,0:T(4,128)(2,1)}), bf16[128,1,4,4,512]{4,3,2,1,0:T(4,128)(2,1)S(1)}, u32[]{:S(2)}, u32[]{:S(2)}) async-start(bf16[128,1,4,4,512]{4,3,2,1,0:T(4,128)(2,1)} %get-tuple-element.18), calls=%async_computation.1 | async-start | bytes 4194304 | tf_op jit(solution)/shard_map/all_to_all | solution.py:53
  44.3 226.2 %all-gather.4.cloned.1.call-start = ((), (), s32[]{:S(2)}) async-start(), calls=%async_computation.6 | async-start | bytes 3604480 | tf_op jit(solution)/shard_map/all_gather | solution.py:135
  97.2 12.0 %copy-start.5 = (bf16[256,512]{1,0:T(8,128)(2,1)S(1)}, bf16[256,512]{1,0:T(8,128)(2,1)}, u32[]{:S(2)}) copy-start(bf16[256,512]{1,0:T(8,128)(2,1)} %param.15) | copy-start | bytes 786436
  97.2 62.7 %all-to-all-start = ((bf16[128,1,4,4,512]{4,3,2,1,0:T(4,128)(2,1)}), bf16[128,1,4,4,512]{4,3,2,1,0:T(4,128)(2,1)}, u32[]{:S(2)}, u32[]{:S(2)}) async-start(bf16[128,1,4,4,512]{4,3,2,1,0:T(4,128)(2,1)} %get-tuple-element.17), calls=%async_computation | async-start | bytes 4194304 | tf_op jit(solution)/shard_map/all_to_all | solution.py:54
  108.5 1.4 copy-start.6
  108.5 4.3 %copy-start.9 = (f32[4]{0:T(128)S(1)}, f32[4]{0:T(128)}, u32[]{:S(2)}) copy-start(f32[4]{0:T(128)} %param.18) | copy-start | bytes 52
  108.5 166.9 %all-gather.6.cloned.1.call-start = ((), (), s32[]{:S(2)}) async-start(), calls=%async_computation.7 | async-start | bytes 3604480 | tf_op jit(solution)/shard_map/all_gather | solution.py:136
  166.4 1.8 copy-start.3
  166.4 11.1 %copy-start.8 = (f32[512]{0:T(512)S(1)}, f32[512]{0:T(512)}, u32[]{:S(2)}) copy-start(f32[512]{0:T(512)} %param.20) | copy-start | bytes 6148
  168.1 231.8 %copy-start.2 = (bf16[256,512]{1,0:T(8,128)(2,1)}, bf16[256,512]{1,0:T(8,128)(2,1)S(1)}, u32[]{:S(2)}) copy-start(bf16[256,512]{1,0:T(8,128)(2,1)S(1)} %copy.107) | copy-start | bytes 786436
  179.7 61.8 %all-to-all-start.2 = ((bf16[128,1,12,512]{3,2,1,0:T(8,128)(2,1)}), bf16[128,1,12,512]{3,2,1,0:T(8,128)(2,1)S(1)}, u32[]{:S(2)}, u32[]{:S(2)}) async-start(bf16[128,1,12,512]{3,2,1,0:T(8,128)(2,1)} %bitcast.136), calls=%async_computation.2 | async-start | bytes 4194304 | tf_op jit(solution)/shard_map/all_to_all | solution.py:128
  188.6 86.8 %all-gather.8.cloned.1.call-start = ((), (), s32[]{:S(2)}) async-start(), calls=%async_computation.8 | async-start | bytes 3604480 | tf_op jit(solution)/shard_map/all_gather | solution.py:137
  350.9 7.4 %copy-start.7 = (f32[256,2]{0,1:T(2,128)S(1)}, f32[256,2]{0,1:T(2,128)}, u32[]{:S(2)}) copy-start(f32[256,2]{0,1:T(2,128)} %param.22) | copy-start | bytes 6148
  351.0 31.3 %all-to-all-start.5 = ((bf16[128,1,3,2048]{0,2,1,3:T(4,128)(2,1)}), bf16[128,1,3,2048]{0,2,1,3:T(4,128)(2,1)S(1)}, u32[]{:S(2)}, u32[]{:S(2)}) async-start(bf16[128,1,3,2048]{0,2,1,3:T(4,128)(2,1)} %copy.104), calls=%async_computation.5 | async-start | bytes 4194304 | tf_op jit(solution)/shard_map/all_to_all | solution.py:145
  394.7 6.1 %copy-start.1 = (bf16[64,4,512]{2,1,0:T(4,128)(2,1)S(1)}, bf16[64,4,512]{2,1,0:T(4,128)(2,1)}, u32[]{:S(2)}) copy-start(bf16[64,4,512]{2,1,0:T(4,128)(2,1)} %param.17) | copy-start | bytes 786436
Sparse Core Ops, SparseCore 0:
  47.2 54.8 all-gather.3
  111.4 55.4 all-gather.5
  191.5 54.8 all-gather.7
where the time goes:
time: 408 us; the launch traced here: 407 us
  waiting for transfers between devices  174 us (43%)
  blocking collectives  97.8 us (24%)
  starting transfers between devices  47.7 us (12%)
  local copies, waits for them, and re-layouts  40.4 us (10%)
  matrix products  18.7 us (5%)
  other arithmetic  14.4 us (4%)
  between operations  14.2 us (3%)
    all_to_all x1, blocking collectives, per_device(): lax.all_to_all(produced, 'ctx', split_axis=0, concat_axis=0, tiled=True)  64.2 us
    all_to_all x1, waiting for transfers between devices, per_device(): lax.all_to_all(outgoing, 'ctx', split_axis=0, concat_axis=0, tiled=True)  52.2 us
    all_to_all x1, waiting for transfers between devices, attend_whole(): lax.all_to_all(send_keys, 'ctx', split_axis=0, concat_axis=0, tiled=True)  52.2 us
    all_to_all x1, waiting for transfers between devices, attend_whole(): lax.all_to_all(send_values, 'ctx', split_axis=0, concat_axis=0, tiled=True)  44.8 us
    all_to_all x1, blocking collectives, per_device(): lax.all_to_all(lax.all_to_all(outgoing, 'ctx', split_axis=0, concat_axis=...  24.4 us
    all_to_all x1, waiting for transfers between devices, per_device(): lax.all_to_all(lax.all_to_all(produced, 'ctx', split_axis=0, concat_axis=...  23.1 us
    all_to_all x1, starting transfers between devices, attend_whole(): lax.all_to_all(send_keys, 'ctx', split_axis=0, concat_axis=0, tiled=True)  20.8 us
    all_to_all x1, starting transfers between devices, attend_whole(): lax.all_to_all(send_values, 'ctx', split_axis=0, concat_axis=0, tiled=True)  11.2 us
  transfers between devices with their start and end apart: 7, of which 4 were waited for; matrix products, arithmetic and copies ran while one was open for 7% of the time, Pallas kernels for 0%

commit v1 on v0

v1 whole, which is shorter than its diff:
```python
import functools
import math

import jax
import jax.numpy as jnp
from jax import lax
from jax.experimental import pallas as pl
from jax.experimental.pallas import tpu as pltpu
from jax.sharding import PartitionSpec as P

D = 2048
EXPERTS = 64
CAP = 12
N = 128
GROUPS = 4
MESH = pl.DeviceIdType.MESH
F32 = jnp.float32
BF16 = jnp.bfloat16

NT = (((1,), (1,)), ((), ()))


def unit_heads(x):
    parts = []
    for h in range(x.shape[1] // 128):
        s = x[:, 128 * h : 128 * (h + 1)].astype(F32)
        parts.append(s * lax.rsqrt(jnp.mean(s * s, axis=1, keepdims=True) + 1e-06))
    return jnp.concatenate(parts, axis=1).astype(BF16)


def layer_kernel(
    mult_ref,
    hid_ref,
    q_ref,
    k_ref,
    v_ref,
    src_ref,
    gain_ref,
    ids_ref,
    share_ref,
    gate_ref,
    up_ref,
    down_ref,
    att_ref,
    mix_ref,
    kvs,
    kvr,
    qbuf,
    qsend,
    hbuf,
    gbuf,
    obuf,
    osend,
    acc,
    den,
    disp,
    comb_hi,
    comb_lo,
    rows32,
    dsend,
    drecv,
    xbuf,
    act,
    rsend,
    rrecv,
    ysend,
    yrecv,
    wg,
    wu,
    wd,
    sems,
    kv_sem,
):
    me = lax.axis_index("ctx")
    f = lax.axis_index("exp")
    i = lax.rem(me, 2)
    nb = me + 1 - 2 * i
    f1 = f + 1 - 2 * lax.rem(f, 2)
    f2 = lax.rem(f + 2, 4)
    f3 = 3 - f
    (KVS, QS, QR, HS, HR, GS, GR, OS, OR, DS, DR, RS, RR, YS, YR, WS, WX, WC, WF, WFS, WT, LOCW) = range(22)

    bar = pltpu.get_barrier_semaphore()

    def greet(k, carry):
        pl.semaphore_signal(bar, inc=1, device_id=(lax.rem(me + k, N), f), device_id_type=MESH)
        return carry

    lax.fori_loop(1, N, greet, 0)
    for g in (f1, f2, f3):
        pl.semaphore_signal(bar, inc=1, device_id=(me, g), device_id_type=MESH)
        pl.semaphore_signal(bar, inc=1, device_id=(nb, g), device_id_type=MESH)

    pick = (lax.broadcasted_iota(jnp.int32, (256, 1024), 0) == src_ref[...]).astype(F32)
    pick = jnp.transpose(pick).astype(BF16)
    kunit = unit_heads(k_ref[...])
    for half in range(2):
        cols = slice(256 * half, 256 * (half + 1))
        got = jnp.dot(pick, kunit[:, cols], preferred_element_type=F32).astype(BF16)
        kvs[:, half, 0:16, :] = got.reshape(64, 16, 256)
        got = jnp.dot(pick, v_ref[:, cols], preferred_element_type=F32).astype(BF16)
        kvs[:, half, 16:32, :] = got.reshape(64, 16, 256)
    qunit = unit_heads(q_ref[...])
    first = jnp.broadcast_to(i, (256, 256)) == 0
    qbuf[i] = jnp.where(first, qunit[:, :256], qunit[:, 256:])
    qsend[...] = jnp.where(first, qunit[:, 256:], qunit[:, :256])

    pl.semaphore_wait(bar, N - 1 + 6)

    def remote(src, dst, s, r, ctx, ex):
        return pltpu.make_async_remote_copy(
            src, dst, sems.at[s], r, device_id=(ctx, ex), device_id_type=MESH
        )

    def wait(ref, sem):
        pltpu.make_async_copy(ref, ref, sem).wait()

    remote(qsend, qbuf.at[i], QS, sems.at[QR], nb, f).start()
    own_kv = pltpu.make_async_copy(kvs.at[me // 2, i], kvr.at[0], kv_sem.at[0])
    own_kv.start()

    def send_kv(k, carry):
        d = lax.rem(me + k, N)
        remote(
            kvs.at[d // 2, lax.rem(d, 2)], kvr.at[k], KVS, kv_sem.at[k // (N // GROUPS)], d, f
        ).start()
        return carry

    lax.fori_loop(1, N // GROUPS, send_kv, 0)

    own_rows = pl.ds(pl.multiple_of(f * 176, 16), 176)
    for g, left, sem in ((f2, WS, WX), (f1, WT, WC)):
        remote(gate_ref.at[0], wg.at[own_rows], left, sems.at[sem], me, g).start()
        remote(up_ref.at[0], wu.at[own_rows], left, sems.at[sem], me, g).start()
        remote(down_ref.at[0], wd.at[f], left, sems.at[sem], me, g).start()
    local_w = [
        pltpu.make_async_copy(gate_ref.at[0], wg.at[own_rows], sems.at[LOCW]),
        pltpu.make_async_copy(up_ref.at[0], wu.at[own_rows], sems.at[LOCW]),
        pltpu.make_async_copy(down_ref.at[0], wd.at[f], sems.at[LOCW]),
    ]
    for c in local_w:
        c.start()
    lax.fori_loop(N // GROUPS, N, send_kv, 0)

    for g in (f1, f2, f3):
        remote(hid_ref, hbuf.at[f], HS, sems.at[HR], me, g).start()
        remote(gain_ref, gbuf.at[f], GS, sems.at[GR], me, g).start()
    hbuf[f] = hid_ref[...]
    gbuf[f] = gain_ref[...]

    ids = ids_ref[...]
    experts = lax.broadcasted_iota(jnp.int32, (EXPERTS, 256), 0)
    named = [(experts == ids[c : c + 1, :]).astype(F32) for c in range(2)]
    counts = (named[0] + named[1]).astype(BF16)
    earlier = (
        lax.broadcasted_iota(jnp.int32, (256, 256), 0) < lax.broadcasted_iota(jnp.int32, (256, 256), 1)
    ).astype(F32).astype(BF16)
    before = jnp.dot(counts, earlier, preferred_element_type=F32)
    keys = []
    for c in range(2):
        rank = jnp.sum(named[c] * before, axis=0, keepdims=True)
        keys.append(ids[c : c + 1, :] * CAP + rank.astype(jnp.int32))
    row = lax.broadcasted_iota(jnp.int32, (192, 256), 0)
    expert = (row * 171) // 512
    slot = expert * CAP + (row - expert * 3)
    mine = slot + 3 * f
    disp[...] = ((keys[0] == mine) | (keys[1] == mine)).astype(F32).astype(BF16)
    for g in range(4):
        there = slot + 3 * g
        table = jnp.where(keys[0] == there, share_ref[0:1, :], 0.0) + jnp.where(
            keys[1] == there, share_ref[1:2, :], 0.0
        )
        high = table.astype(BF16).astype(F32)
        comb_hi[g] = jnp.transpose(high).astype(BF16)
        comb_lo[g] = jnp.transpose(table - high).astype(BF16)

    acc[...] = jnp.zeros_like(acc)
    den[...] = jnp.zeros_like(den)
    wait(qbuf.at[0], sems.at[QR])
    per = N // GROUPS

    def attend(grp, carry):
        wait(kvr.at[pl.ds(0, per)], kv_sem.at[grp])
        span = pl.ds(pl.multiple_of(grp * per, per), per)
        kg = kvr[span, 0:16, :].reshape(per * 16, 256)
        vg = kvr[span, 16:32, :].reshape(per * 16, 256)
        for h in range(2):
            cols = slice(128 * h, 128 * (h + 1))
            scale = mult_ref[2 * i + h] * (1.0 / math.sqrt(128.0))
            for j in range(2):
                s = lax.dot_general(qbuf[j, :, cols], kg[:, cols], NT, preferred_element_type=F32)
                e = jnp.exp(s * scale)
                total = e[:, 0:128]
                for c in range(1, per * 16 // 128):
                    total = total + e[:, 128 * c : 128 * (c + 1)]
                den[j, h] += total
                acc[j, h] += jnp.dot(e.astype(BF16), vg[:, cols], preferred_element_type=F32)
        return carry

    lax.fori_loop(0, GROUPS, attend, 0)
    for j in range(2):
        for h in range(2):
            out = acc[j, h] / jnp.sum(den[j, h], axis=1, keepdims=True)
            osend[j, :, 128 * h : 128 * (h + 1)] = out.astype(BF16)

    mark = 2 * f + i
    for g in (f1, f2, f3):
        remote(osend.at[i], obuf.at[mark], OS, sems.at[OR], me, g).start()
    for g in (f, f1, f2, f3):
        remote(osend.at[1 - i], obuf.at[mark], OS, sems.at[OR], nb, g).start()
    obuf[mark] = osend[i]
    wait(hbuf.at[pl.ds(0, 3)], sems.at[HR])
    wait(gbuf.at[pl.ds(0, 3)], sems.at[GR])
    wait(obuf.at[pl.ds(0, 7)], sems.at[OR])

    squares = jnp.zeros((256, 1), F32)
    for s in range(8):
        cols = slice(256 * (s % 2), 256 * (s % 2) + 256)
        part = hbuf[s // 2, :, cols].astype(F32) + obuf[s].astype(F32)
        squares = squares + jnp.sum(part * part, axis=1, keepdims=True)
    inverse = lax.rsqrt(squares / D + 1e-05)
    for s in range(8):
        cols = slice(256 * (s % 2), 256 * (s % 2) + 256)
        part = hbuf[s // 2, :, cols].astype(F32) + obuf[s].astype(F32)
        unit = (part * inverse * gbuf[s // 2, 0:1, cols]).astype(BF16)
        sent = jnp.dot(disp[...], unit, preferred_element_type=F32)
        for c in range(2):
            rows32[pl.ds(2 * s + c, 192, stride=16), :] = sent[:, 128 * c : 128 * (c + 1)]
    for b in range(8):
        dsend[pl.ds(8 * b, 8)] = rows32[pl.ds(384 * b, 384), :].astype(BF16).reshape(8, 48, 128)

    own_d = pltpu.make_async_copy(dsend.at[me // 2], drecv.at[0], sems.at[DR])
    own_d.start()

    def send_rows(k, carry):
        d = lax.rem(me + k, N)
        remote(dsend.at[d // 2], drecv.at[k], DS, sems.at[DR], d, f).start()
        return carry

    lax.fori_loop(1, N, send_rows, 0)

    three = pl.ds(0, 528)
    wait(wg.at[three], sems.at[WX])
    rows2 = pl.ds(pl.multiple_of(f2 * 176, 16), 176)
    remote(wg.at[rows2], wg.at[rows2], WFS, sems.at[WF], me, f1).start()
    remote(wu.at[rows2], wu.at[rows2], WFS, sems.at[WF], me, f1).start()
    remote(wd.at[f2], wd.at[f2], WFS, sems.at[WF], me, f1).start()
    wait(wg.at[three], sems.at[LOCW])
    wait(wg.at[three], sems.at[WC])
    wait(wg.at[three], sems.at[WF])

    wait(drecv, sems.at[DR])

    def widen(b, carry):
        rows32[pl.ds(pl.multiple_of(384 * b, 384), 384), :] = (
            drecv[pl.ds(pl.multiple_of(8 * b, 8), 8)].reshape(384, 128).astype(F32)
        )
        return carry

    lax.fori_loop(0, 16, widen, 0)
    for c in range(16):
        xbuf[:, 128 * c : 128 * (c + 1)] = rows32[pl.ds(c, 384, stride=16), :].astype(BF16)
    for lo, hi in ((0, 256), (256, 512), (512, 704)):
        gate = lax.dot_general(xbuf[...], wg[lo:hi, :], NT, preferred_element_type=F32)
        up = lax.dot_general(xbuf[...], wu[lo:hi, :], NT, preferred_element_type=F32)
        act[:, lo:hi] = (gate / (1.0 + jnp.exp(-gate)) * up).astype(BF16)
    for g in range(4):
        out = jnp.dot(act[...], wd[g], preferred_element_type=F32)
        for c in range(4):
            rows32[pl.ds(4 * g + c, 384, stride=16), :] = out[:, 128 * c : 128 * (c + 1)]

    def narrow(b, carry):
        rsend[pl.ds(pl.multiple_of(8 * b, 8), 8)] = (
            rows32[pl.ds(pl.multiple_of(384 * b, 384), 384), :].astype(BF16).reshape(8, 48, 128)
        )
        return carry

    lax.fori_loop(0, 16, narrow, 0)
    own_r = pltpu.make_async_copy(rsend.at[0], rrecv.at[me], sems.at[RR])
    own_r.start()

    def send_back(k, carry):
        d = lax.rem(me + N - k, N)
        remote(rsend.at[k], rrecv.at[me], RS, sems.at[RR], d, f).start()
        return carry

    lax.fori_loop(1, N, send_back, 0)
    wait(rrecv, sems.at[RR])

    def pieces(b, carry):
        pair = rrecv[pl.ds(pl.multiple_of(16 * b, 16), 16)].astype(F32).reshape(8, 2, 48, 128)
        rows32[pl.ds(pl.multiple_of(384 * b, 384), 384), :] = (pair[:, 0] + pair[:, 1]).reshape(384, 128)
        return carry

    lax.fori_loop(0, 8, pieces, 0)
    for c in range(16):
        ysend[c // 4, :, 128 * (c % 4) : 128 * (c % 4) + 128] = rows32[
            pl.ds(c, 192, stride=16), :
        ].astype(BF16)
    for g in (f2, f3, f1):
        remote(ysend.at[g], yrecv.at[f], YS, sems.at[YR], me, g).start()
    yrecv[f] = ysend[f]
    wait(yrecv.at[pl.ds(0, 3)], sems.at[YR])

    total = jnp.zeros((256, 512), F32)
    for g in range(4):
        total = total + jnp.dot(comb_hi[g], yrecv[g], preferred_element_type=F32)
        total = total + jnp.dot(comb_lo[g], yrecv[g], preferred_element_type=F32)
    for s in range(2):
        cols = slice(256 * s, 256 * (s + 1))
        mine_o = obuf[2 * f + s]
        att_ref[:, cols] = mine_o
        summed = hid_ref[:, cols].astype(F32) + mine_o.astype(F32)
        mix_ref[:, cols] = (summed + total[:, cols]).astype(BF16)

    wait(qsend, sems.at[QS])
    wait(kvr.at[pl.ds(0, N - 1)], sems.at[KVS])
    wait(hbuf.at[pl.ds(0, 3)], sems.at[HS])
    wait(gbuf.at[pl.ds(0, 3)], sems.at[GS])
    wait(obuf.at[pl.ds(0, 7)], sems.at[OS])
    wait(drecv.at[pl.ds(0, N - 1)], sems.at[DS])
    wait(rrecv.at[pl.ds(0, N - 1)], sems.at[RS])
    wait(yrecv.at[pl.ds(0, 3)], sems.at[YS])
    wait(wg.at[three], sems.at[WFS])
    wait(wg.at[three], sems.at[WS])
    wait(wg.at[three], sems.at[WT])


def per_device(
    hidden_state_stream,
    question_vectors,
    memory_lookup_vectors,
    content_vectors,
    logit_multiplier,
    chosen_tile_lists,
    premix_rmsnorm_scaling,
    routing_choice_ids,
    routing_shares,
    gating_matrix,
    raising_matrix,
    lowering_matrix,
):
    src = (chosen_tile_lists[:, :, None] * 4 + jnp.arange(4, dtype=jnp.int32)).reshape(1, 1024)
    gain = jnp.broadcast_to(premix_rmsnorm_scaling[None, :], (8, 512))
    vmem = pl.BlockSpec(memory_space=pltpu.VMEM)
    hbm = pl.BlockSpec(memory_space=pl.ANY)
    scratch = [
        pltpu.VMEM((64, 2, 32, 256), BF16),
        pltpu.VMEM((N, 32, 256), BF16),
        pltpu.VMEM((2, 256, 256), BF16),
        pltpu.VMEM((256, 256), BF16),
        pltpu.VMEM((4, 256, 512), BF16),
        pltpu.VMEM((4, 8, 512), F32),
        pltpu.VMEM((8, 256, 256), BF16),
        pltpu.VMEM((2, 256, 256), BF16),
        pltpu.VMEM((2, 2, 256, 128), F32),
        pltpu.VMEM((2, 2, 256, 128), F32),
        pltpu.VMEM((192, 256), BF16),
        pltpu.VMEM((4, 256, 192), BF16),
        pltpu.VMEM((4, 256, 192), BF16),
        pltpu.VMEM((6144, 128), F32),
        pltpu.VMEM((64, 48, 128), BF16),
        pltpu.VMEM((N, 48, 128), BF16),
        pltpu.VMEM((384, 2048), BF16),
        pltpu.VMEM((384, 704), BF16),
        pltpu.VMEM((N, 48, 128), BF16),
        pltpu.VMEM((N, 48, 128), BF16),
        pltpu.VMEM((4, 192, 512), BF16),
        pltpu.VMEM((4, 192, 512), BF16),
        pltpu.VMEM((704, 2048), BF16),
        pltpu.VMEM((704, 2048), BF16),
        pltpu.VMEM((4, 704, 512), BF16),
        pltpu.SemaphoreType.DMA((22,)),
        pltpu.SemaphoreType.DMA((GROUPS,)),
    ]
    shape = jax.ShapeDtypeStruct((256, 512), BF16)
    return pl.pallas_call(
        layer_kernel,
        out_shape=(shape, shape),
        in_specs=[pl.BlockSpec(memory_space=pltpu.SMEM)] + [vmem] * 8 + [hbm] * 3,
        out_specs=(vmem, vmem),
        scratch_shapes=scratch,
        name="layer",
        cost_estimate=pl.CostEstimate(flops=5_000_000_000, bytes_accessed=20_000_000, transcendentals=3_000_000),
        compiler_params=pltpu.CompilerParams(
            collective_id=1, has_side_effects=True, vmem_limit_bytes=52 * 2**20
        ),
    )(
        logit_multiplier,
        hidden_state_stream,
        question_vectors,
        memory_lookup_vectors.reshape(256, 512),
        content_vectors.reshape(256, 512),
        src,
        gain,
        routing_choice_ids.T,
        routing_shares.T,
        gating_matrix,
        raising_matrix,
        lowering_matrix,
    )


def solution(mesh):
    in_specs = (
        P("ctx", "exp"),
        P("ctx", "exp"),
        P(None, "ctx", "exp"),
        P(None, "ctx", "exp"),
        P("exp"),
        P(),
        P("exp"),
        P("ctx", None),
        P("ctx", None),
        P("ctx", "exp", None),
        P("ctx", "exp", None),
        P("ctx", None, "exp"),
    )
    out_specs = (P("ctx", "exp"), P("ctx", "exp"))
    return jax.shard_map(
        per_device, mesh=mesh, in_specs=in_specs, out_specs=out_specs, check_vma=False
    )
```

time: 408 us -> 221 us (0.54)
  Pallas kernels: 0 us -> 214 us
  waiting for transfers between devices: 174 us -> 0 us
  blocking collectives: 97.8 us -> 0 us
  starting transfers between devices: 47.7 us -> 0 us
  local copies, waits for them, and re-layouts: 40.4 us -> 4.94 us
  matrix products: 18.7 us -> 0 us
  other arithmetic: 14.4 us -> 0.13 us
  between operations: 14.2 us -> 0.73 us
    pallas_call x0 -> x1, Pallas kernels: none -> 214 us  [per_device(): pl.pallas_call(layer_kernel, out_shape=(shape, shape), in_specs=[pl.Block...]
    all_to_all x4 -> x0, waiting for transfers between devices: 172 us -> none  [the longest x1 52.2 us: per_device(): lax.all_to_all(outgoing, 'ctx', split_axis=0, concat_axis=0, tiled=True)]
    all_to_all x2 -> x0, blocking collectives: 88.6 us -> none  [the longest x1 64.2 us: per_device(): lax.all_to_all(produced, 'ctx', split_axis=0, concat_axis=0, tiled=True)]
    all_to_all x4 -> x0, starting transfers between devices: 47.4 us -> none  [the longest x1 20.8 us: attend_whole(): lax.all_to_all(send_keys, 'ctx', split_axis=0, concat_axis=0, tiled=True)]
    dot_general x6 -> x0, matrix products: 18.7 us -> none  [the longest x1 6.51 us: per_device(): jnp.einsum('nplh,phf->nplf', activated, full_down, preferred_element_type...]
    gather x5 -> x0, local copies, waits for them, and re-layouts: 11.9 us -> none  [the longest x2 4.41 us: per_device(): jnp.take(flat_back, targets.reshape(-1), axis=0)]
    all_to_all x4 -> x0, local copies, waits for them, and re-layouts: 9.62 us -> none  [the longest x1 4.06 us: per_device(): lax.all_to_all(lax.all_to_all(produced, 'ctx', split_axis=0, concat_axis=...]
    psum x1 -> x0, blocking collectives: 9.17 us -> none  [per_device(): squares = lax.psum(jnp.sum(summed * summed, axis=1), 'exp')]
  transfers between devices with their start and end apart: 7 -> 0, of which waited for: 4 -> 0; matrix products, arithmetic and copies ran while one was open for 7% -> 0% of each run, Pallas kernels for 0% -> 0%
where the time goes in v1:
time: 221 us; the launch traced here: 219 us
  Pallas kernels  214 us (97%)
  local copies, waits for them, and re-layouts  4.94 us (2%)
    pallas_call x1, Pallas kernels, per_device(): pl.pallas_call(layer_kernel, out_shape=(shape, shape), in_specs=[pl.Block...  214 us

profile of v1, /device:TPU:1, one launch (start us, length us, event | category | flops | bytes accessed | tf_op | source)
XLA Modules:
  0.0 219.4 jit_solution(7826335488366271406)
XLA Ops:
  0.6 0.0 copy-start.7
  0.6 0.0 copy-start.5
  0.6 0.7 copy-done.7
  1.3 0.7 broadcast_in_dim.2.gain_ref
  2.0 0.1 copy.15
  2.1 0.1 iota_add_fusion
  2.2 0.2 add.26.src_ref
  2.4 0.0 copy-done.5
  2.4 0.0 copy-start.6
  2.4 0.0 copy-start.2
  2.4 0.0 copy-start.3
  2.4 0.0 copy-start.4
  2.4 0.1 reshape.36.k_ref
  2.5 0.8 copy-done.6
  3.4 0.0 copy-start
  3.4 0.0 copy-start.1
  3.4 0.1 reshape.37.v_ref
  3.4 0.0 copy-done.2
  3.4 0.0 copy-done.3
  3.4 0.0 copy-done.4
  3.5 0.8 copy-done
  4.3 0.1 copy-done.1
  4.4 213.6 %layer.1 = (bf16[256,512]{1,0:T(8,128)(2,1)S(1)}, bf16[256,512]{1,0:T(8,128)(2,1)S(1)}) custom-call(f32[4]{0:T(128)S(1)} %copy-done.4, bf16[256,512]{1,0:T(8,128)(2,1)S(1)} %copy-done, bf16[256,512]{1,0:T(8,128)(2,1)S(1)} %copy-done.1, bf16[256,512]{1,0:T(8,128)(2,1)S(1)} %reshape.36.k_ref, bf16[256,512]{1,0:T(8,128)(2,1)S(1)} %reshape.37.v_ref, ...), custom_call_target="tpu_custom_call" | custom-call | flops 5000000000 | bytes 20000000 | tf_op jit(solution)/shard_map/layer/pallas_call | solution.py:377
  218.0 0.7 copy.18
  218.7 0.7 copy.19
  (1 shorter events, 0.0 us)
Async XLA Ops:
  0.6 0.7 copy-start.7
  0.6 1.8 copy-start.5
  2.4 1.0 copy-start.6
  2.4 1.0 copy-start.2
  2.4 1.0 copy-start.3
  2.4 1.0 copy-start.4
  3.4 0.9 copy-start
  3.4 1.0 copy-start.1

commit v2 on v1

--- a/solution.py
+++ b/solution.py
@@ -60,16 +60,21 @@
     dsend,
     drecv,
     xbuf,
-    act,
+    abuf,
+    psend,
+    precv,
     rsend,
     rrecv,
-    ysend,
-    yrecv,
+    ybuf,
     wg,
     wu,
     wd,
     sems,
     kv_sem,
+    d_sem,
+    fwd_sem,
+    p_sem,
+    a_sem,
 ):
     me = lax.axis_index("ctx")
     f = lax.axis_index("exp")
@@ -78,7 +83,12 @@
     f1 = f + 1 - 2 * lax.rem(f, 2)
     f2 = lax.rem(f + 2, 4)
     f3 = 3 - f
-    (KVS, QS, QR, HS, HR, GS, GR, OS, OR, DS, DR, RS, RR, YS, YR, WS, WX, WC, WF, WFS, WT, LOCW) = range(22)
+    mz = lax.rem(me, 8)
+    my = lax.rem(me // 8, 8)
+    mx = me // 64
+    zp = mz // 2
+    (KVS, QS, QR, HS, HX, HC, HF, HFS, GS, GR, OS, OR, DS, FS, PS, RS, RR) = range(17)
+    (WS, WX, WT, WC, WF, WFS, US, UX, UT, UC, UF, UFS, LOCW) = range(17, 30)
 
     bar = pltpu.get_barrier_semaphore()
 
@@ -100,10 +110,6 @@
         kvs[:, half, 0:16, :] = got.reshape(64, 16, 256)
         got = jnp.dot(pick, v_ref[:, cols], preferred_element_type=F32).astype(BF16)
         kvs[:, half, 16:32, :] = got.reshape(64, 16, 256)
-    qunit = unit_heads(q_ref[...])
-    first = jnp.broadcast_to(i, (256, 256)) == 0
-    qbuf[i] = jnp.where(first, qunit[:, :256], qunit[:, 256:])
-    qsend[...] = jnp.where(first, qunit[:, 256:], qunit[:, :256])
 
     pl.semaphore_wait(bar, N - 1 + 6)
 
@@ -115,7 +121,6 @@
     def wait(ref, sem):
         pltpu.make_async_copy(ref, ref, sem).wait()
 
-    remote(qsend, qbuf.at[i], QS, sems.at[QR], nb, f).start()
     own_kv = pltpu.make_async_copy(kvs.at[me // 2, i], kvr.at[0], kv_sem.at[0])
     own_kv.start()
 
@@ -128,22 +133,29 @@
 
     lax.fori_loop(1, N // GROUPS, send_kv, 0)
 
-    own_rows = pl.ds(pl.multiple_of(f * 176, 16), 176)
+    def shard(who, lo, hi):
+        return pl.ds(pl.multiple_of(who * 176 + lo, 16), hi - lo)
+
     for g, left, sem in ((f2, WS, WX), (f1, WT, WC)):
-        remote(gate_ref.at[0], wg.at[own_rows], left, sems.at[sem], me, g).start()
-        remote(up_ref.at[0], wu.at[own_rows], left, sems.at[sem], me, g).start()
-        remote(down_ref.at[0], wd.at[f], left, sems.at[sem], me, g).start()
-    local_w = [
-        pltpu.make_async_copy(gate_ref.at[0], wg.at[own_rows], sems.at[LOCW]),
-        pltpu.make_async_copy(up_ref.at[0], wu.at[own_rows], sems.at[LOCW]),
-        pltpu.make_async_copy(down_ref.at[0], wd.at[f], sems.at[LOCW]),
-    ]
-    for c in local_w:
+        remote(gate_ref.at[0], wg.at[shard(f, 0, 176)], left, sems.at[sem], me, g).start()
+        remote(up_ref.at[0, 0:96], wu.at[shard(f, 0, 96)], left, sems.at[sem], me, g).start()
+    for c in (
+        pltpu.make_async_copy(gate_ref.at[0], wg.at[shard(f, 0, 176)], sems.at[LOCW]),
+        pltpu.make_async_copy(up_ref.at[0], wu.at[shard(f, 0, 176)], sems.at[LOCW]),
+        pltpu.make_async_copy(down_ref.at[0], wd, sems.at[LOCW]),
+    ):
         c.start()
     lax.fori_loop(N // GROUPS, N, send_kv, 0)
 
+    qunit = unit_heads(q_ref[...])
+    first = jnp.broadcast_to(i, (256, 256)) == 0
+    qbuf[i] = jnp.where(first, qunit[:, :256], qunit[:, 256:])
+    qsend[...] = jnp.where(first, qunit[:, 256:], qunit[:, :256])
+    remote(qsend, qbuf.at[i], QS, sems.at[QR], nb, f).start()
+
+    for g, sem in ((f2, HX), (f1, HC)):
+        remote(hid_ref, hbuf.at[f], HS, sems.at[sem], me, g).start()
     for g in (f1, f2, f3):
-        remote(hid_ref, hbuf.at[f], HS, sems.at[HR], me, g).start()
         remote(gain_ref, gbuf.at[f], GS, sems.at[GR], me, g).start()
     hbuf[f] = hid_ref[...]
     gbuf[f] = gain_ref[...]
@@ -165,14 +177,17 @@
     slot = expert * CAP + (row - expert * 3)
     mine = slot + 3 * f
     disp[...] = ((keys[0] == mine) | (keys[1] == mine)).astype(F32).astype(BF16)
-    for g in range(4):
-        there = slot + 3 * g
+    for b in range(3):
+        line = lax.broadcasted_iota(jnp.int32, (256, 256), 0) + 256 * b
+        expert = (line * 5462) // 65536
+        inner = line - expert * 12
+        there = expert * CAP + 3 * lax.rem(inner, 4) + inner // 4
         table = jnp.where(keys[0] == there, share_ref[0:1, :], 0.0) + jnp.where(
             keys[1] == there, share_ref[1:2, :], 0.0
         )
         high = table.astype(BF16).astype(F32)
-        comb_hi[g] = jnp.transpose(high).astype(BF16)
-        comb_lo[g] = jnp.transpose(table - high).astype(BF16)
+        comb_hi[:, 256 * b : 256 * (b + 1)] = jnp.transpose(high).astype(BF16)
+        comb_lo[:, 256 * b : 256 * (b + 1)] = jnp.transpose(table - high).astype(BF16)
 
     acc[...] = jnp.zeros_like(acc)
     den[...] = jnp.zeros_like(den)
@@ -203,13 +218,20 @@
             out = acc[j, h] / jnp.sum(den[j, h], axis=1, keepdims=True)
             osend[j, :, 128 * h : 128 * (h + 1)] = out.astype(BF16)
 
+    wait(hbuf.at[0], sems.at[HX])
+    remote(hbuf.at[f2], hbuf.at[f2], HFS, sems.at[HF], me, f1).start()
     mark = 2 * f + i
     for g in (f1, f2, f3):
         remote(osend.at[i], obuf.at[mark], OS, sems.at[OR], me, g).start()
     for g in (f, f1, f2, f3):
         remote(osend.at[1 - i], obuf.at[mark], OS, sems.at[OR], nb, g).start()
     obuf[mark] = osend[i]
-    wait(hbuf.at[pl.ds(0, 3)], sems.at[HR])
+    early = pl.ds(0, 272)
+    wait(wg.at[early], sems.at[WX])
+    remote(wg.at[shard(f2, 0, 176)], wg.at[shard(f2, 0, 176)], WFS, sems.at[WF], me, f1).start()
+    remote(wu.at[shard(f2, 0, 96)], wu.at[shard(f2, 0, 96)], WFS, sems.at[WF], me, f1).start()
+    wait(hbuf.at[0], sems.at[HC])
+    wait(hbuf.at[0], sems.at[HF])
     wait(gbuf.at[pl.ds(0, 3)], sems.at[GR])
     wait(obuf.at[pl.ds(0, 7)], sems.at[OR])
 
@@ -229,83 +251,151 @@
     for b in range(8):
         dsend[pl.ds(8 * b, 8)] = rows32[pl.ds(384 * b, 384), :].astype(BF16).reshape(8, 48, 128)
 
-    own_d = pltpu.make_async_copy(dsend.at[me // 2], drecv.at[0], sems.at[DR])
+    def near(q, sign):
+        x = lax.rem(mx + 2 + sign * lax.rem(q, 2), 2)
+        y = lax.rem(my + 8 + sign * (q // 2), 8)
+        return x * 64 + y * 8
+
+    def send_rows(q, kinds):
+        column = near(q, 1)
+        for off, member, slot_ in (
+            (0, i, 0),
+            (1, 0, 1 + i),
+            (3, 1, 1 + i),
+            (2, 1 - i, 3),
+        )[kinds]:
+            pair = lax.rem(zp + off, 4)
+            remote(
+                dsend.at[column // 2 + pair],
+                drecv.at[1, 4 * q + slot_],
+                DS,
+                d_sem.at[q // 4],
+                column + 2 * pair + member,
+                f,
+            ).start()
+
+    own_d = pltpu.make_async_copy(dsend.at[me // 2], drecv.at[1, 0], d_sem.at[0])
     own_d.start()
-
-    def send_rows(k, carry):
-        d = lax.rem(me + k, N)
-        remote(dsend.at[d // 2], drecv.at[k], DS, sems.at[DR], d, f).start()
-        return carry
-
-    lax.fori_loop(1, N, send_rows, 0)
-
-    three = pl.ds(0, 528)
-    wait(wg.at[three], sems.at[WX])
-    rows2 = pl.ds(pl.multiple_of(f2 * 176, 16), 176)
-    remote(wg.at[rows2], wg.at[rows2], WFS, sems.at[WF], me, f1).start()
-    remote(wu.at[rows2], wu.at[rows2], WFS, sems.at[WF], me, f1).start()
-    remote(wd.at[f2], wd.at[f2], WFS, sems.at[WF], me, f1).start()
-    wait(wg.at[three], sems.at[LOCW])
-    wait(wg.at[three], sems.at[WC])
-    wait(wg.at[three], sems.at[WF])
-
-    wait(drecv, sems.at[DR])
-
-    def widen(b, carry):
+    send_rows(0, slice(1, 4))
+
+    def send_column(q, carry):
+        send_rows(q, slice(0, 4))
+        return carry
+
+    lax.fori_loop(1, 16, send_column, 0)
+
+    for g, left, sem in ((f2, US, UX), (f1, UT, UC)):
+        remote(up_ref.at[0, 96:176], wu.at[shard(f, 96, 176)], left, sems.at[sem], me, g).start()
+
+    def pass_on(g, carry):
+        span = pl.ds(pl.multiple_of(16 * g, 16), 16)
+        wait(drecv.at[1, pl.ds(0, 16)], d_sem.at[g])
+        remote(drecv.at[1, span], drecv.at[0, span], FS, fwd_sem.at[g], nb, f).start()
+        return carry
+
+    lax.fori_loop(0, 4, pass_on, 0)
+
+    late = pl.ds(0, 80)
+    wait(wg.at[late], sems.at[UX])
+    remote(wu.at[shard(f2, 96, 176)], wu.at[shard(f2, 96, 176)], UFS, sems.at[UF], me, f1).start()
+    wait(wg.at[pl.ds(0, 528)], sems.at[LOCW])
+    wait(wg.at[early], sems.at[WC])
+    wait(wg.at[early], sems.at[WF])
+    wait(wg.at[late], sems.at[UC])
+    wait(wg.at[late], sems.at[UF])
+
+    def hidden(half):
+        def widen(b, carry):
+            rows32[pl.ds(pl.multiple_of(384 * b, 384), 384), :] = (
+                drecv[half, pl.ds(pl.multiple_of(8 * b, 8), 8)].reshape(384, 128).astype(F32)
+            )
+            return carry
+
+        lax.fori_loop(0, 8, widen, 0)
+        for c in range(16):
+            xbuf[:, 128 * c : 128 * (c + 1)] = rows32[pl.ds(c, 192, stride=16), :].astype(BF16)
+        for lo, hi in ((0, 256), (256, 512), (512, 704)):
+            gate = lax.dot_general(xbuf[...], wg[lo:hi, :], NT, preferred_element_type=F32)
+            up = lax.dot_general(xbuf[...], wu[lo:hi, :], NT, preferred_element_type=F32)
+            abuf[half, f, :, lo:hi] = (gate / (1.0 + jnp.exp(-gate)) * up).astype(BF16)
+        here = abuf.at[half, f]
+        remote(here, here, 6 * half + 30, a_sem.at[half, 0], me, f2).start()
+        remote(here, here, 6 * half + 31, a_sem.at[half, 1], me, f1).start()
+
+    def share_on(half):
+        there = abuf.at[half, f2]
+        wait(there, a_sem.at[half, 0])
+        remote(there, there, 6 * half + 32, a_sem.at[half, 2], me, f1).start()
+
+    def lower(half):
+        for s in (1, 2):
+            wait(abuf.at[half, 0], a_sem.at[half, s])
+        for g in range(4):
+            out = jnp.dot(abuf[half, g], wd[...], preferred_element_type=F32)
+            for c in range(4):
+                rows32[pl.ds(4 * g + c, 192, stride=16), :] = out[:, 128 * c : 128 * (c + 1)]
+
+    hidden(1)
+    share_on(1)
+    for g in range(4):
+        wait(drecv.at[0, pl.ds(0, 16)], fwd_sem.at[g])
+    hidden(0)
+    share_on(0)
+    lower(0)
+
+    def partner(g, carry):
+        span = pl.ds(pl.multiple_of(16 * g, 16), 16)
+        psend[span] = (
+            rows32[pl.ds(pl.multiple_of(768 * g, 768), 768), :].astype(BF16).reshape(16, 48, 128)
+        )
+        remote(psend.at[span], precv.at[span], PS, p_sem.at[g], nb, f).start()
+        return carry
+
+    lax.fori_loop(0, 4, partner, 0)
+    lower(1)
+
+    def send_back(q, kinds):
+        column = near(q, -1)
+        side = 2 * lax.rem(zp + 3 + 2 * i, 4)
+        for slot_, z in ((0, mz), (1, side), (2, side + 1), (3, 2 * lax.rem(zp + 2, 4) + 1 - i))[kinds]:
+            remote(rsend.at[4 * q + slot_], rrecv.at[me // 2], RS, sems.at[RR], column + z, f).start()
+
+    def pair_sum(g):
+        span = pl.ds(pl.multiple_of(16 * g, 16), 16)
+        wait(precv.at[pl.ds(0, 16)], p_sem.at[g])
+        own = rows32[pl.ds(pl.multiple_of(768 * g, 768), 768), :].astype(BF16).astype(F32)
+        other = precv[span].reshape(768, 128).astype(F32)
+        rsend[span] = (own + other).astype(BF16).reshape(16, 48, 128)
+
+    def back_column(q, carry):
+        send_back(q, slice(0, 4))
+        return carry
+
+    pair_sum(0)
+    own_r = pltpu.make_async_copy(rsend.at[0], rrecv.at[me // 2], sems.at[RR])
+    own_r.start()
+    send_back(0, slice(1, 4))
+    lax.fori_loop(1, 4, back_column, 0)
+
+    def back_group(g, carry):
+        pair_sum(g)
+        lax.fori_loop(4 * g, 4 * g + 4, back_column, 0)
+        return carry
+
+    lax.fori_loop(1, 4, back_group, 0)
+    wait(rrecv, sems.at[RR])
+
+    def widen_back(b, carry):
         rows32[pl.ds(pl.multiple_of(384 * b, 384), 384), :] = (
-            drecv[pl.ds(pl.multiple_of(8 * b, 8), 8)].reshape(384, 128).astype(F32)
+            rrecv[pl.ds(pl.multiple_of(8 * b, 8), 8)].reshape(384, 128).astype(F32)
         )
         return carry
 
-    lax.fori_loop(0, 16, widen, 0)
-    for c in range(16):
-        xbuf[:, 128 * c : 128 * (c + 1)] = rows32[pl.ds(c, 384, stride=16), :].astype(BF16)
-    for lo, hi in ((0, 256), (256, 512), (512, 704)):
-        gate = lax.dot_general(xbuf[...], wg[lo:hi, :], NT, preferred_element_type=F32)
-        up = lax.dot_general(xbuf[...], wu[lo:hi, :], NT, preferred_element_type=F32)
-        act[:, lo:hi] = (gate / (1.0 + jnp.exp(-gate)) * up).astype(BF16)
-    for g in range(4):
-        out = jnp.dot(act[...], wd[g], preferred_element_type=F32)
-        for c in range(4):
-            rows32[pl.ds(4 * g + c, 384, stride=16), :] = out[:, 128 * c : 128 * (c + 1)]
-
-    def narrow(b, carry):
-        rsend[pl.ds(pl.multiple_of(8 * b, 8), 8)] = (
-            rows32[pl.ds(pl.multiple_of(384 * b, 384), 384), :].astype(BF16).reshape(8, 48, 128)
-        )
-        return carry
-
-    lax.fori_loop(0, 16, narrow, 0)
-    own_r = pltpu.make_async_copy(rsend.at[0], rrecv.at[me], sems.at[RR])
-    own_r.start()
-
-    def send_back(k, carry):
-        d = lax.rem(me + N - k, N)
-        remote(rsend.at[k], rrecv.at[me], RS, sems.at[RR], d, f).start()
-        return carry
-
-    lax.fori_loop(1, N, send_back, 0)
-    wait(rrecv, sems.at[RR])
-
-    def pieces(b, carry):
-        pair = rrecv[pl.ds(pl.multiple_of(16 * b, 16), 16)].astype(F32).reshape(8, 2, 48, 128)
-        rows32[pl.ds(pl.multiple_of(384 * b, 384), 384), :] = (pair[:, 0] + pair[:, 1]).reshape(384, 128)
-        return carry
-
-    lax.fori_loop(0, 8, pieces, 0)
-    for c in range(16):
-        ysend[c // 4, :, 128 * (c % 4) : 128 * (c % 4) + 128] = rows32[
-            pl.ds(c, 192, stride=16), :
-        ].astype(BF16)
-    for g in (f2, f3, f1):
-        remote(ysend.at[g], yrecv.at[f], YS, sems.at[YR], me, g).start()
-    yrecv[f] = ysend[f]
-    wait(yrecv.at[pl.ds(0, 3)], sems.at[YR])
-
-    total = jnp.zeros((256, 512), F32)
-    for g in range(4):
-        total = total + jnp.dot(comb_hi[g], yrecv[g], preferred_element_type=F32)
-        total = total + jnp.dot(comb_lo[g], yrecv[g], preferred_element_type=F32)
+    lax.fori_loop(0, 8, widen_back, 0)
+    for c in range(4):
+        ybuf[:, 128 * c : 128 * (c + 1)] = rows32[pl.ds(c, 768, stride=4), :].astype(BF16)
+    total = jnp.dot(comb_hi[...], ybuf[...], preferred_element_type=F32)
+    total = total + jnp.dot(comb_lo[...], ybuf[...], preferred_element_type=F32)
     for s in range(2):
         cols = slice(256 * s, 256 * (s + 1))
         mine_o = obuf[2 * f + s]
@@ -315,15 +405,21 @@
 
     wait(qsend, sems.at[QS])
     wait(kvr.at[pl.ds(0, N - 1)], sems.at[KVS])
-    wait(hbuf.at[pl.ds(0, 3)], sems.at[HS])
+    wait(hbuf.at[pl.ds(0, 2)], sems.at[HS])
+    wait(hbuf.at[0], sems.at[HFS])
     wait(gbuf.at[pl.ds(0, 3)], sems.at[GS])
     wait(obuf.at[pl.ds(0, 7)], sems.at[OS])
-    wait(drecv.at[pl.ds(0, N - 1)], sems.at[DS])
-    wait(rrecv.at[pl.ds(0, N - 1)], sems.at[RS])
-    wait(yrecv.at[pl.ds(0, 3)], sems.at[YS])
-    wait(wg.at[three], sems.at[WFS])
-    wait(wg.at[three], sems.at[WS])
-    wait(wg.at[three], sems.at[WT])
+    wait(rrecv.at[pl.ds(0, 63)], sems.at[DS])
+    wait(drecv.at[0], sems.at[FS])
+    wait(precv, sems.at[PS])
+    wait(rrecv.at[pl.ds(0, 63)], sems.at[RS])
+    for s in (WS, WT, WFS):
+        wait(wg.at[early], sems.at[s])
+    for s in (US, UT, UFS):
+        wait(wg.at[late], sems.at[s])
+    for half in range(2):
+        for s in range(3):
+            wait(abuf.at[half, 0], sems.at[30 + 6 * half + s])
 
 
 def per_device(
@@ -356,22 +452,27 @@
         pltpu.VMEM((2, 2, 256, 128), F32),
         pltpu.VMEM((2, 2, 256, 128), F32),
         pltpu.VMEM((192, 256), BF16),
-        pltpu.VMEM((4, 256, 192), BF16),
-        pltpu.VMEM((4, 256, 192), BF16),
-        pltpu.VMEM((6144, 128), F32),
+        pltpu.VMEM((256, 768), BF16),
+        pltpu.VMEM((256, 768), BF16),
+        pltpu.VMEM((3072, 128), F32),
         pltpu.VMEM((64, 48, 128), BF16),
-        pltpu.VMEM((N, 48, 128), BF16),
-        pltpu.VMEM((384, 2048), BF16),
-        pltpu.VMEM((384, 704), BF16),
-        pltpu.VMEM((N, 48, 128), BF16),
-        pltpu.VMEM((N, 48, 128), BF16),
-        pltpu.VMEM((4, 192, 512), BF16),
-        pltpu.VMEM((4, 192, 512), BF16),
+        pltpu.VMEM((2, 64, 48, 128), BF16),
+        pltpu.VMEM((192, 2048), BF16),
+        pltpu.VMEM((2, 4, 192, 704), BF16),
+        pltpu.VMEM((64, 48, 128), BF16),
+        pltpu.VMEM((64, 48, 128), BF16),
+        pltpu.VMEM((64, 48, 128), BF16),
+        pltpu.VMEM((64, 48, 128), BF16),
+        pltpu.VMEM((768, 512), BF16),
         pltpu.VMEM((704, 2048), BF16),
         pltpu.VMEM((704, 2048), BF16),
-        pltpu.VMEM((4, 704, 512), BF16),
-        pltpu.SemaphoreType.DMA((22,)),
+        pltpu.VMEM((704, 512), BF16),
+        pltpu.SemaphoreType.DMA((40,)),
         pltpu.SemaphoreType.DMA((GROUPS,)),
+        pltpu.SemaphoreType.DMA((4,)),
+        pltpu.SemaphoreType.DMA((4,)),
+        pltpu.SemaphoreType.DMA((4,)),
+        pltpu.SemaphoreType.DMA((2, 3)),
     ]
     shape = jax.ShapeDtypeStruct((256, 512), BF16)
     return pl.pallas_call(

time: 221 us -> 186 us (0.84)
  Pallas kernels: 214 us -> 180 us
    pallas_call x1, Pallas kernels: 214 us -> 180 us  [per_device(): pl.pallas_call(layer_kernel, out_shape=(shape, shape), in_specs=[pl.Block...]
where the time goes in v2:
time: 186 us; the launch traced here: 185 us
  Pallas kernels  180 us (97%)
  local copies, waits for them, and re-layouts  4.94 us (3%)
    pallas_call x1, Pallas kernels, per_device(): pl.pallas_call(layer_kernel, out_shape=(shape, shape), in_specs=[pl.Block...  180 us
    unnamed x18, local copies, waits for them, and re-layouts  3.87 us

profile of v2, /device:TPU:1, one launch (start us, length us, event | category | flops | bytes accessed | tf_op | source)
XLA Modules:
  0.0 185.4 jit_solution(5138535743395282022)
XLA Ops:
  0.6 0.0 copy-start.7
  0.6 0.0 copy-start.5
  0.6 0.7 copy-done.7
  1.3 0.7 broadcast_in_dim.2.gain_ref
  2.0 0.1 copy.15
  2.1 0.1 iota_add_fusion
  2.2 0.2 add.26.src_ref
  2.4 0.0 copy-done.5
  2.4 0.0 copy-start.6
  2.4 0.0 copy-start.2
  2.4 0.0 copy-start.3
  2.4 0.0 copy-start.4
  2.4 0.1 reshape.36.k_ref
  2.5 0.8 copy-done.6
  3.4 0.0 copy-start
  3.4 0.0 copy-start.1
  3.4 0.1 reshape.37.v_ref
  3.4 0.0 copy-done.2
  3.4 0.0 copy-done.3
  3.4 0.0 copy-done.4
  3.5 0.8 copy-done
  4.3 0.1 copy-done.1
  4.4 179.6 %layer.1 = (bf16[256,512]{1,0:T(8,128)(2,1)S(1)}, bf16[256,512]{1,0:T(8,128)(2,1)S(1)}) custom-call(f32[4]{0:T(128)S(1)} %copy-done.4, bf16[256,512]{1,0:T(8,128)(2,1)S(1)} %copy-done, bf16[256,512]{1,0:T(8,128)(2,1)S(1)} %copy-done.1, bf16[256,512]{1,0:T(8,128)(2,1)S(1)} %reshape.36.k_ref, bf16[256,512]{1,0:T(8,128)(2,1)S(1)} %reshape.37.v_ref, ...), custom_call_target="tpu_custom_call" | custom-call | flops 5000000000 | bytes 20000000 | tf_op jit(solution)/shard_map/layer/pallas_call | solution.py:478
  184.0 0.7 copy.18
  184.7 0.7 copy.19
  (1 shorter events, 0.0 us)
Async XLA Ops:
  0.6 0.7 copy-start.7
  0.6 1.8 copy-start.5
  2.4 1.0 copy-start.6
  2.4 1.0 copy-start.2
  2.4 1.0 copy-start.3
  2.4 1.0 copy-start.4
  3.4 0.9 copy-start
  3.4 1.0 copy-start.1

commit v3 on v2

v3 whole, which is shorter than its diff:
```python
import functools
import math

import jax
import jax.numpy as jnp
from jax import lax
from jax.experimental import pallas as pl
from jax.experimental.pallas import tpu as pltpu
from jax.sharding import PartitionSpec as P

D = 2048
EXPERTS = 64
CAP = 12
N = 128
OWN = 40
MESH = pl.DeviceIdType.MESH
F32 = jnp.float32
BF16 = jnp.bfloat16

NT = (((1,), (1,)), ((), ()))


def unit_heads(x):
    parts = []
    for h in range(x.shape[1] // 128):
        s = x[:, 128 * h : 128 * (h + 1)].astype(F32)
        parts.append(s * lax.rsqrt(jnp.mean(s * s, axis=1, keepdims=True) + 1e-06))
    return jnp.concatenate(parts, axis=1).astype(BF16)


def layer_kernel(
    mult_ref,
    hid_ref,
    q_ref,
    k_ref,
    v_ref,
    src_ref,
    gain_ref,
    ids_ref,
    share_ref,
    gate_ref,
    up_ref,
    down_ref,
    att_ref,
    mix_ref,
    kvs,
    mid_a,
    mid_b,
    kvr_a,
    kvr_b,
    qbuf,
    qsend,
    hbuf,
    gbuf,
    obuf,
    osend,
    acc,
    den,
    disp,
    comb_hi,
    comb_lo,
    rows32,
    part32,
    dsend,
    drecv,
    xbuf,
    abuf_a,
    abuf_b,
    psend,
    precv,
    rsend,
    rrecv,
    ybuf,
    wg,
    wu,
    wd,
    sems,
    kva_sem,
    kvb_sem,
    d_sem,
    ds_sem,
    fwd_sem,
    p_sem,
    a_sem,
):
    me = lax.axis_index("ctx")
    f = lax.axis_index("exp")
    i = lax.rem(me, 2)
    nb = me + 1 - 2 * i
    f1 = f + 1 - 2 * lax.rem(f, 2)
    f2 = lax.rem(f + 2, 4)
    f3 = 3 - f
    mz = lax.rem(me, 8)
    my = lax.rem(me // 8, 8)
    mx = me // 64
    zp = mz // 2
    xy = me // 8
    (QS, QR, HS, HX, HC, HF, HFS, GS, GR, OS, OR, DS, FS, PS, RS, RR, OX, OY, OZ, OFS, K1, K2, K3, K4, KA, KB, KL, KM) = range(16 + 12)
    (WS, WX, WT, WC, WF, WFS, US, UX, UT, UC, UF, UFS, LOCW) = range(28, 41)
    AS = 41

    bar = pltpu.get_barrier_semaphore()

    def greet(k, carry):
        pl.semaphore_signal(bar, inc=1, device_id=(lax.rem(me + k, N), f), device_id_type=MESH)
        return carry

    lax.fori_loop(1, N, greet, 0)
    for g in (f1, f2, f3):
        pl.semaphore_signal(bar, inc=1, device_id=(me, g), device_id_type=MESH)
        pl.semaphore_signal(bar, inc=1, device_id=(nb, g), device_id_type=MESH)

    pick = (lax.broadcasted_iota(jnp.int32, (256, 1024), 0) == src_ref[...]).astype(F32)
    pick = jnp.transpose(pick).astype(BF16)
    kunit = unit_heads(k_ref[...])
    for half in range(2):
        for head in range(2):
            cols = slice(256 * half + 128 * head, 256 * half + 128 * head + 128)
            got = jnp.dot(pick, kunit[:, cols], preferred_element_type=F32).astype(BF16)
            kvs[:, :, half, head, 0:16, :] = got.reshape(16, 4, 16, 128)
            got = jnp.dot(pick, v_ref[:, cols], preferred_element_type=F32).astype(BF16)
            kvs[:, :, half, head, 16:32, :] = got.reshape(16, 4, 16, 128)

    pl.semaphore_wait(bar, N - 1 + 6)

    def remote(src, dst, s, r, ctx, ex):
        left = sems.at[s] if isinstance(s, int) else s
        return pltpu.make_async_remote_copy(
            src, dst, left, r, device_id=(ctx, ex), device_id_type=MESH
        )

    def wait(ref, sem):
        pltpu.make_async_copy(ref, ref, sem).wait()

    def ring(k):
        return xy * 8 + lax.rem(mz + k, 8)

    def column(k):
        return lax.rem(xy + k, 16) * 8 + mz

    def first_z(k):
        d = lax.rem(mz + k, 8)
        src = kvs.at[:, d // 2, lax.rem(d, 2), 0]
        remote(src, mid_a.at[mz], K3, sems.at[KA], ring(k), f).start()

    def first_xy(k):
        d = lax.rem(xy + k, 16)
        remote(kvs.at[d, :, :, 1], mid_b.at[xy], K1, sems.at[KB], column(k), f).start()

    def first_step(k, carry):
        first_z(k)
        first_xy(2 * k - 1)
        first_xy(2 * k)
        return carry

    lax.fori_loop(1, 8, first_step, 0)
    first_xy(15)
    own_a = pltpu.make_async_copy(kvs.at[:, mz // 2, lax.rem(mz, 2), 0], mid_a.at[mz], sems.at[KM])
    own_a.start()
    own_b = pltpu.make_async_copy(kvs.at[xy, :, :, 1], mid_b.at[xy], sems.at[KL])
    own_b.start()

    def shard(who, lo, hi):
        return pl.ds(pl.multiple_of(who * 176 + lo, 16), hi - lo)

    for g, left, sem in ((f2, WS, WX), (f1, WT, WC)):
        remote(gate_ref.at[0], wg.at[shard(f, 0, 176)], left, sems.at[sem], me, g).start()
    for c in (
        pltpu.make_async_copy(gate_ref.at[0], wg.at[shard(f, 0, 176)], sems.at[LOCW]),
        pltpu.make_async_copy(up_ref.at[0], wu.at[shard(f, 0, 176)], sems.at[LOCW]),
        pltpu.make_async_copy(down_ref.at[0], wd, sems.at[LOCW]),
    ):
        c.start()

    qunit = unit_heads(q_ref[...])
    first = jnp.broadcast_to(i, (256, 256)) == 0
    qbuf[i] = jnp.where(first, qunit[:, :256], qunit[:, 256:])
    qsend[...] = jnp.where(first, qunit[:, 256:], qunit[:, :256])
    remote(qsend, qbuf.at[i], QS, sems.at[QR], nb, f).start()

    for g, sem in ((f2, HX), (f1, HC)):
        remote(hid_ref, hbuf.at[f], HS, sems.at[sem], me, g).start()
    for g in (f1, f2, f3):
        remote(gain_ref, gbuf.at[f], GS, sems.at[GR], me, g).start()
    hbuf[f] = hid_ref[...]
    gbuf[f] = gain_ref[...]

    ids = ids_ref[...]
    experts = lax.broadcasted_iota(jnp.int32, (EXPERTS, 256), 0)
    named = [(experts == ids[c : c + 1, :]).astype(F32) for c in range(2)]
    counts = (named[0] + named[1]).astype(BF16)
    earlier = (
        lax.broadcasted_iota(jnp.int32, (256, 256), 0) < lax.broadcasted_iota(jnp.int32, (256, 256), 1)
    ).astype(F32).astype(BF16)
    before = jnp.dot(counts, earlier, preferred_element_type=F32)
    keys = []
    for c in range(2):
        rank = jnp.sum(named[c] * before, axis=0, keepdims=True)
        keys.append(ids[c : c + 1, :] * CAP + rank.astype(jnp.int32))
    row = lax.broadcasted_iota(jnp.int32, (192, 256), 0)
    expert = (row * 171) // 512
    slot = expert * CAP + (row - expert * 3)
    mine = slot + 3 * f
    disp[...] = ((keys[0] == mine) | (keys[1] == mine)).astype(F32).astype(BF16)
    for b in range(3):
        line = lax.broadcasted_iota(jnp.int32, (256, 256), 0) + 256 * b
        expert = (line * 5462) // 65536
        inner = line - expert * 12
        there = expert * CAP + 3 * lax.rem(inner, 4) + inner // 4
        table = jnp.where(keys[0] == there, share_ref[0:1, :], 0.0) + jnp.where(
            keys[1] == there, share_ref[1:2, :], 0.0
        )
        high = table.astype(BF16).astype(F32)
        comb_hi[:, 256 * b : 256 * (b + 1)] = jnp.transpose(high).astype(BF16)
        comb_lo[:, 256 * b : 256 * (b + 1)] = jnp.transpose(table - high).astype(BF16)

    own_a.wait()
    own_b.wait()
    wait(mid_a.at[pl.ds(0, 7)], sems.at[KA])
    own_a = pltpu.make_async_copy(mid_a.at[:, xy], kvr_a.at[0], kva_sem.at[0])
    own_a.start()

    def second_xy(k, carry):
        d = lax.rem(xy + k, 16)
        remote(mid_a.at[:, d], kvr_a.at[k], K2, kva_sem.at[k // 4], column(k), f).start()
        return carry

    lax.fori_loop(1, 16, second_xy, 0)
    wait(mid_b.at[pl.ds(0, 15)], sems.at[KB])
    own_b = pltpu.make_async_copy(mid_b.at[:, mz // 2, lax.rem(mz, 2)], kvr_b.at[0], kvb_sem.at[0])
    own_b.start()

    def second_z(k, carry):
        d = lax.rem(mz + k, 8)
        remote(
            mid_b.at[:, d // 2, lax.rem(d, 2)], kvr_b.at[k], K4, kvb_sem.at[k // 2], ring(k), f
        ).start()
        return carry

    lax.fori_loop(1, 8, second_z, 0)

    acc[...] = jnp.zeros_like(acc)
    den[...] = jnp.zeros_like(den)
    wait(qbuf.at[0], sems.at[QR])

    def attend(h, kg, vg):
        cols = slice(128 * h, 128 * (h + 1))
        scale = mult_ref[2 * i + h] * (1.0 / math.sqrt(128.0))
        for j in range(2):
            s = lax.dot_general(qbuf[j, :, cols], kg, NT, preferred_element_type=F32)
            e = jnp.exp(s * scale)
            total = e[:, 0:128]
            for c in range(1, 4):
                total = total + e[:, 128 * c : 128 * (c + 1)]
            den[j, h] += total
            acc[j, h] += jnp.dot(e.astype(BF16), vg, preferred_element_type=F32)

    def attend_group(g, carry):
        wait(kvr_a.at[pl.ds(0, 4)], kva_sem.at[g])
        span = pl.ds(pl.multiple_of(4 * g, 4), 4)
        attend(0, kvr_a[span, :, 0:16, :].reshape(512, 128), kvr_a[span, :, 16:32, :].reshape(512, 128))
        wait(kvr_b.at[pl.ds(0, 2)], kvb_sem.at[g])
        span = pl.ds(pl.multiple_of(2 * g, 2), 2)
        attend(1, kvr_b[span, :, 0:16, :].reshape(512, 128), kvr_b[span, :, 16:32, :].reshape(512, 128))
        return carry

    lax.fori_loop(0, 4, attend_group, 0)
    for j in range(2):
        for h in range(2):
            out = acc[j, h] / jnp.sum(den[j, h], axis=1, keepdims=True)
            osend[j, :, 128 * h : 128 * (h + 1)] = out.astype(BF16)

    wait(hbuf.at[0], sems.at[HX])
    remote(hbuf.at[f2], hbuf.at[f2], HFS, sems.at[HF], me, f1).start()
    mark = 2 * f + i
    for src, ctx, sem in ((i, me, OX), (1 - i, nb, OY)):
        remote(osend.at[src], obuf.at[mark], OS, sems.at[sem], ctx, f2).start()
    remote(osend.at[1 - i], obuf.at[mark], OS, sems.at[OZ], nb, f).start()
    remote(osend.at[i], obuf.at[mark], OS, sems.at[OR], me, f1).start()
    obuf[mark] = osend[i]
    for who, sem in ((2 * f + 1 - i, OZ), (2 * f2 + i, OX), (2 * f2 + 1 - i, OY)):
        wait(obuf.at[0], sems.at[sem])
        remote(obuf.at[who], obuf.at[who], OFS, sems.at[OR], me, f1).start()
    early = pl.ds(0, 176)
    wait(wg.at[early], sems.at[WX])
    remote(wg.at[shard(f2, 0, 176)], wg.at[shard(f2, 0, 176)], WFS, sems.at[WF], me, f1).start()
    wait(hbuf.at[0], sems.at[HC])
    wait(hbuf.at[0], sems.at[HF])
    wait(gbuf.at[pl.ds(0, 3)], sems.at[GR])
    wait(obuf.at[pl.ds(0, 4)], sems.at[OR])

    for g, left, sem in ((f2, US, UX), (f1, UT, UC)):
        remote(up_ref.at[0], wu.at[shard(f, 0, 176)], left, sems.at[sem], me, g).start()

    squares = jnp.zeros((256, 1), F32)
    for s in range(8):
        cols = slice(256 * (s % 2), 256 * (s % 2) + 256)
        part = hbuf[s // 2, :, cols].astype(F32) + obuf[s].astype(F32)
        squares = squares + jnp.sum(part * part, axis=1, keepdims=True)
    inverse = lax.rsqrt(squares / D + 1e-05)
    for s in range(8):
        cols = slice(256 * (s % 2), 256 * (s % 2) + 256)
        part = hbuf[s // 2, :, cols].astype(F32) + obuf[s].astype(F32)
        unit = (part * inverse * gbuf[s // 2, 0:1, cols]).astype(BF16)
        sent = jnp.dot(disp[...], unit, preferred_element_type=F32)
        for c in range(2):
            rows32[pl.ds(2 * s + c, 192, stride=16), :] = sent[:, 128 * c : 128 * (c + 1)]
    for b in range(8):
        dsend[pl.ds(8 * b, 8)] = rows32[pl.ds(384 * b, 384), :].astype(BF16).reshape(8, 48, 128)

    steps = ((3, 5), (2, 6), (4, 0), (1, 7))

    def near(g, m, sign):
        low, high = steps[g]
        x = lax.rem(mx + m, 2)
        y = lax.rem(my + 8 + sign * (low + (high - low) * (m // 2)), 8)
        return x * 64 + y * 8

    def send_rows(g, m, kinds):
        column_ = near(g, m, 1)
        for off, member, slot_ in (
            (0, i, 0),
            (1, 0, 1 + i),
            (3, 1, 1 + i),
            (2, 1 - i, 3),
        )[kinds]:
            pair = lax.rem(zp + off, 4)
            remote(
                dsend.at[column_ // 2 + pair],
                drecv.at[1, 16 * g + 4 * m + slot_],
                ds_sem.at[g],
                d_sem.at[g],
                column_ + 2 * pair + member,
                f,
            ).start()

    def send_group(g, each):
        def one(m, carry):
            each(g, m, slice(0, 4))
            return carry

        if 0 in steps[g]:
            lax.fori_loop(0, 2, one, 0)
            each(g, 2, slice(1, 4))
            each(g, 3, slice(0, 4))
        else:
            lax.fori_loop(0, 4, one, 0)

    own_d = pltpu.make_async_copy(dsend.at[me // 2], drecv.at[1, OWN], d_sem.at[OWN // 16])
    own_d.start()
    send_group(0, send_rows)
    send_group(1, send_rows)
    for g in range(4):
        span = pl.ds(16 * g, 16)
        wait(drecv.at[1, span], d_sem.at[g])
        remote(drecv.at[1, span], drecv.at[0, span], FS, fwd_sem.at[g], nb, f).start()
        if g < 2:
            wait(drecv.at[1, pl.ds(0, 16)], ds_sem.at[g])
            send_group(g + 2, send_rows)

    wait(wg.at[early], sems.at[UX])
    remote(wu.at[shard(f2, 0, 176)], wu.at[shard(f2, 0, 176)], UFS, sems.at[UF], me, f1).start()
    wait(wg.at[pl.ds(0, 528)], sems.at[LOCW])
    wait(wg.at[early], sems.at[WC])
    wait(wg.at[early], sems.at[WF])
    wait(wg.at[early], sems.at[UC])
    wait(wg.at[early], sems.at[UF])

    def hidden(part_, kind, first_slot, rows, mine_buf):
        def widen(b, carry):
            rows32[pl.ds(pl.multiple_of(384 * b, 384), 384), :] = (
                drecv[kind, pl.ds(pl.multiple_of(first_slot + 8 * b, 8), 8)].reshape(384, 128).astype(F32)
            )
            return carry

        lax.fori_loop(0, rows // 24, widen, 0)
        for c in range(16):
            xbuf[0:rows, 128 * c : 128 * (c + 1)] = rows32[pl.ds(c, rows, stride=16), :].astype(BF16)
        x = xbuf[0:rows, :]
        for lo, hi in ((0, 256), (256, 512), (512, 704)):
            gate = lax.dot_general(x, wg[lo:hi, :], NT, preferred_element_type=F32)
            up = lax.dot_general(x, wu[lo:hi, :], NT, preferred_element_type=F32)
            mine_buf[f, :, lo:hi] = (gate / (1.0 + jnp.exp(-gate)) * up).astype(BF16)
        here = mine_buf.at[f]
        remote(here, here, AS + 3 * part_, a_sem.at[part_, 0], me, f2).start()
        remote(here, here, AS + 3 * part_ + 1, a_sem.at[part_, 1], me, f1).start()

    def share_on(part_, buf):
        wait(buf.at[0], a_sem.at[part_, 0])
        remote(buf.at[f2], buf.at[f2], AS + 3 * part_ + 2, a_sem.at[part_, 2], me, f1).start()

    def lower(part_, buf, rows, out32):
        for s in (1, 2):
            wait(buf.at[0], a_sem.at[part_, s])
        for g in range(4):
            out = jnp.dot(buf[g], wd[...], preferred_element_type=F32)
            for c in range(4):
                out32[pl.ds(4 * g + c, rows, stride=16), :] = out[:, 128 * c : 128 * (c + 1)]

    def partner(first_group):
        for g in range(2):
            span = pl.ds(16 * (first_group + g), 16)
            psend[span] = part32[768 * g : 768 * (g + 1), :].astype(BF16).reshape(16, 48, 128)
            remote(psend.at[span], precv.at[span], PS, p_sem.at[first_group + g], nb, f).start()

    part_b, part_c = abuf_b.at[0], abuf_b.at[1]
    hidden(0, 1, 0, 192, abuf_a)
    for g in range(2):
        wait(drecv.at[0, pl.ds(0, 16)], fwd_sem.at[g])
    hidden(1, 0, 0, 96, part_b)
    share_on(0, abuf_a)
    share_on(1, part_b)
    for g in range(2, 4):
        wait(drecv.at[0, pl.ds(0, 16)], fwd_sem.at[g])
    hidden(2, 0, 32, 96, part_c)
    lower(1, part_b, 96, part32)
    partner(0)
    lower(0, abuf_a, 192, rows32)
    share_on(2, part_c)
    lower(2, part_c, 96, part32)
    partner(2)

    def send_back(g, m, kinds):
        column_ = near(g, m, -1)
        side = 2 * lax.rem(zp + 3 + 2 * i, 4)
        for slot_, z in ((0, mz), (1, side), (2, side + 1), (3, 2 * lax.rem(zp + 2, 4) + 1 - i))[kinds]:
            remote(
                rsend.at[16 * g + 4 * m + slot_], rrecv.at[me // 2], RS, sems.at[RR], column_ + z, f
            ).start()

    for g in range(4):
        span = pl.ds(16 * g, 16)
        wait(precv.at[span], p_sem.at[g])
        own = rows32[768 * g : 768 * (g + 1), :].astype(BF16).astype(F32)
        other = precv[span].reshape(768, 128).astype(F32)
        rsend[span] = (own + other).astype(BF16).reshape(16, 48, 128)
        if g == OWN // 16:
            own_r = pltpu.make_async_copy(rsend.at[OWN], rrecv.at[me // 2], sems.at[RR])
            own_r.start()
        send_group(g, send_back)
    wait(rrecv, sems.at[RR])

    def widen_back(b, carry):
        rows32[pl.ds(pl.multiple_of(384 * b, 384), 384), :] = (
            rrecv[pl.ds(pl.multiple_of(8 * b, 8), 8)].reshape(384, 128).astype(F32)
        )
        return carry

    lax.fori_loop(0, 8, widen_back, 0)
    for c in range(4):
        ybuf[:, 128 * c : 128 * (c + 1)] = rows32[pl.ds(c, 768, stride=4), :].astype(BF16)
    total = jnp.dot(comb_hi[...], ybuf[...], preferred_element_type=F32)
    total = total + jnp.dot(comb_lo[...], ybuf[...], preferred_element_type=F32)
    for s in range(2):
        cols = slice(256 * s, 256 * (s + 1))
        mine_o = obuf[2 * f + s]
        att_ref[:, cols] = mine_o
        summed = hid_ref[:, cols].astype(F32) + mine_o.astype(F32)
        mix_ref[:, cols] = (summed + total[:, cols]).astype(BF16)

    wait(qsend, sems.at[QS])
    wait(kvr_a.at[pl.ds(0, 15)], sems.at[K1])
    wait(kvr_a.at[pl.ds(0, 15)], sems.at[K2])
    wait(kvr_b.at[pl.ds(0, 7)], sems.at[K3])
    wait(kvr_b.at[pl.ds(0, 7)], sems.at[K4])
    wait(hbuf.at[pl.ds(0, 2)], sems.at[HS])
    wait(hbuf.at[0], sems.at[HFS])
    wait(gbuf.at[pl.ds(0, 3)], sems.at[GS])
    wait(obuf.at[pl.ds(0, 4)], sems.at[OS])
    wait(obuf.at[pl.ds(0, 3)], sems.at[OFS])
    wait(rrecv.at[pl.ds(0, 15)], ds_sem.at[2])
    wait(rrecv.at[pl.ds(0, 16)], ds_sem.at[3])
    wait(drecv.at[0], sems.at[FS])
    wait(precv, sems.at[PS])
    wait(rrecv.at[pl.ds(0, 63)], sems.at[RS])
    for s in (WS, WT, WFS):
        wait(wg.at[early], sems.at[s])
    for s in (US, UT, UFS):
        wait(wg.at[early], sems.at[s])
    for s in range(3):
        wait(abuf_a.at[0], sems.at[AS + s])
        wait(abuf_b.at[0, 0], sems.at[AS + 3 + s])
        wait(abuf_b.at[0, 0], sems.at[AS + 6 + s])


def per_device(
    hidden_state_stream,
    question_vectors,
    memory_lookup_vectors,
    content_vectors,
    logit_multiplier,
    chosen_tile_lists,
    premix_rmsnorm_scaling,
    routing_choice_ids,
    routing_shares,
    gating_matrix,
    raising_matrix,
    lowering_matrix,
):
    src = (chosen_tile_lists[:, :, None] * 4 + jnp.arange(4, dtype=jnp.int32)).reshape(1, 1024)
    gain = jnp.broadcast_to(premix_rmsnorm_scaling[None, :], (8, 512))
    vmem = pl.BlockSpec(memory_space=pltpu.VMEM)
    hbm = pl.BlockSpec(memory_space=pl.ANY)
    scratch = [
        pltpu.VMEM((16, 4, 2, 2, 32, 128), BF16),
        pltpu.VMEM((8, 16, 32, 128), BF16),
        pltpu.VMEM((16, 4, 2, 32, 128), BF16),
        pltpu.VMEM((16, 8, 32, 128), BF16),
        pltpu.VMEM((8, 16, 32, 128), BF16),
        pltpu.VMEM((2, 256, 256), BF16),
        pltpu.VMEM((256, 256), BF16),
        pltpu.VMEM((4, 256, 512), BF16),
        pltpu.VMEM((4, 8, 512), F32),
        pltpu.VMEM((8, 256, 256), BF16),
        pltpu.VMEM((2, 256, 256), BF16),
        pltpu.VMEM((2, 2, 256, 128), F32),
        pltpu.VMEM((2, 2, 256, 128), F32),
        pltpu.VMEM((192, 256), BF16),
        pltpu.VMEM((256, 768), BF16),
        pltpu.VMEM((256, 768), BF16),
        pltpu.VMEM((3072, 128), F32),
        pltpu.VMEM((1536, 128), F32),
        pltpu.VMEM((64, 48, 128), BF16),
        pltpu.VMEM((2, 64, 48, 128), BF16),
        pltpu.VMEM((192, 2048), BF16),
        pltpu.VMEM((4, 192, 704), BF16),
        pltpu.VMEM((2, 4, 96, 704), BF16),
        pltpu.VMEM((64, 48, 128), BF16),
        pltpu.VMEM((64, 48, 128), BF16),
        pltpu.VMEM((64, 48, 128), BF16),
        pltpu.VMEM((64, 48, 128), BF16),
        pltpu.VMEM((768, 512), BF16),
        pltpu.VMEM((704, 2048), BF16),
        pltpu.VMEM((704, 2048), BF16),
        pltpu.VMEM((704, 512), BF16),
        pltpu.SemaphoreType.DMA((50,)),
        pltpu.SemaphoreType.DMA((4,)),
        pltpu.SemaphoreType.DMA((4,)),
        pltpu.SemaphoreType.DMA((4,)),
        pltpu.SemaphoreType.DMA((4,)),
        pltpu.SemaphoreType.DMA((4,)),
        pltpu.SemaphoreType.DMA((4,)),
        pltpu.SemaphoreType.DMA((3, 3)),
    ]
    shape = jax.ShapeDtypeStruct((256, 512), BF16)
    return pl.pallas_call(
        layer_kernel,
        out_shape=(shape, shape),
        in_specs=[pl.BlockSpec(memory_space=pltpu.SMEM)] + [vmem] * 8 + [hbm] * 3,
        out_specs=(vmem, vmem),
        scratch_shapes=scratch,
        name="layer",
        cost_estimate=pl.CostEstimate(flops=5_000_000_000, bytes_accessed=20_000_000, transcendentals=3_000_000),
        compiler_params=pltpu.CompilerParams(
            collective_id=1, has_side_effects=True, vmem_limit_bytes=52 * 2**20
        ),
    )(
        logit_multiplier,
        hidden_state_stream,
        question_vectors,
        memory_lookup_vectors.reshape(256, 512),
        content_vectors.reshape(256, 512),
        src,
        gain,
        routing_choice_ids.T,
        routing_shares.T,
        gating_matrix,
        raising_matrix,
        lowering_matrix,
    )


def solution(mesh):
    in_specs = (
        P("ctx", "exp"),
        P("ctx", "exp"),
        P(None, "ctx", "exp"),
        P(None, "ctx", "exp"),
        P("exp"),
        P(),
        P("exp"),
        P("ctx", None),
        P("ctx", None),
        P("ctx", "exp", None),
        P("ctx", "exp", None),
        P("ctx", None, "exp"),
    )
    out_specs = (P("ctx", "exp"), P("ctx", "exp"))
    return jax.shard_map(
        per_device, mesh=mesh, in_specs=in_specs, out_specs=out_specs, check_vma=False
    )
```

time: 186 us -> 166 us (0.89)
  Pallas kernels: 180 us -> 160 us
    pallas_call x1, Pallas kernels: 180 us -> 160 us  [per_device(): pl.pallas_call(layer_kernel, out_shape=(shape, shape), in_specs=[pl.Block...]
where the time goes in v3:
time: 166 us
  Pallas kernels  160 us (96%)
  local copies, waits for them, and re-layouts  4.94 us (3%)
    pallas_call x1, Pallas kernels, per_device(): pl.pallas_call(layer_kernel, out_shape=(shape, shape), in_specs=[pl.Block...  160 us
    unnamed x18, local copies, waits for them, and re-layouts  3.87 us

profile of v3, /device:TPU:1, one launch (start us, length us, event | category | flops | bytes accessed | tf_op | source)
XLA Modules:
  0.0 165.8 jit_solution(6435425431994884756)
XLA Ops:
  0.6 0.0 copy-start.7
  0.6 0.0 copy-start.5
  0.6 0.7 copy-done.7
  1.3 0.7 broadcast_in_dim.2.gain_ref
  2.0 0.1 copy.15
  2.1 0.1 iota_add_fusion
  2.2 0.2 add.26.src_ref
  2.4 0.0 copy-done.5
  2.4 0.0 copy-start.6
  2.4 0.0 copy-start.2
  2.4 0.0 copy-start.3
  2.4 0.0 copy-start.4
  2.4 0.1 reshape.36.k_ref
  2.5 0.8 copy-done.6
  3.4 0.0 copy-start
  3.4 0.0 copy-start.1
  3.4 0.1 reshape.37.v_ref
  3.4 0.0 copy-done.2
  3.4 0.0 copy-done.3
  3.4 0.0 copy-done.4
  3.5 0.8 copy-done
  4.3 0.1 copy-done.1
  4.4 160.0 %layer.1 = (bf16[256,512]{1,0:T(8,128)(2,1)S(1)}, bf16[256,512]{1,0:T(8,128)(2,1)S(1)}) custom-call(f32[4]{0:T(128)S(1)} %copy-done.4, bf16[256,512]{1,0:T(8,128)(2,1)S(1)} %copy-done, bf16[256,512]{1,0:T(8,128)(2,1)S(1)} %copy-done.1, bf16[256,512]{1,0:T(8,128)(2,1)S(1)} %reshape.36.k_ref, bf16[256,512]{1,0:T(8,128)(2,1)S(1)} %reshape.37.v_ref, ...), custom_call_target="tpu_custom_call" | custom-call | flops 5000000000 | bytes 20000000 | tf_op jit(solution)/shard_map/layer/pallas_call | solution.py:546
  164.4 0.7 copy.18
  165.1 0.7 copy.19
  (1 shorter events, 0.0 us)
Async XLA Ops:
  0.6 0.7 copy-start.7
  0.6 1.8 %copy-start.5 = (bf16[64,4,512]{2,1,0:T(4,128)(2,1)S(1)}, bf16[64,4,512]{2,1,0:T(4,128)(2,1)}, u32[]{:S(2)}) copy-start(bf16[64,4,512]{2,1,0:T(4,128)(2,1)} %param.14) | copy-start | bytes 786436
  2.4 1.0 copy-start.6
  2.4 1.0 copy-start.2
  2.4 1.0 copy-start.3
  2.4 1.0 copy-start.4
  3.4 0.9 copy-start
  3.4 1.0 copy-start.1

commit v4 on v3

--- a/solution.py
+++ b/solution.py
@@ -48,6 +48,7 @@
     mid_b,
     kvr_a,
     kvr_b,
+    qown,
     qbuf,
     qsend,
     hbuf,
@@ -61,6 +62,7 @@
     comb_lo,
     rows32,
     part32,
+    wide32,
     dsend,
     drecv,
     xbuf,
@@ -82,6 +84,7 @@
     fwd_sem,
     p_sem,
     a_sem,
+    in_sem,
 ):
     me = lax.axis_index("ctx")
     f = lax.axis_index("exp")
@@ -99,6 +102,11 @@
     (WS, WX, WT, WC, WF, WFS, US, UX, UT, UC, UF, UFS, LOCW) = range(28, 41)
     AS = 41
 
+    own_q = pltpu.make_async_copy(q_ref, qown, in_sem.at[0])
+    own_q.start()
+    own_h = pltpu.make_async_copy(hid_ref, hbuf.at[f], in_sem.at[1])
+    own_h.start()
+
     bar = pltpu.get_barrier_semaphore()
 
     def greet(k, carry):
@@ -172,17 +180,18 @@
     ):
         c.start()
 
-    qunit = unit_heads(q_ref[...])
+    own_q.wait()
+    own_h.wait()
+    qunit = unit_heads(qown[...])
     first = jnp.broadcast_to(i, (256, 256)) == 0
     qbuf[i] = jnp.where(first, qunit[:, :256], qunit[:, 256:])
     qsend[...] = jnp.where(first, qunit[:, 256:], qunit[:, :256])
     remote(qsend, qbuf.at[i], QS, sems.at[QR], nb, f).start()
 
     for g, sem in ((f2, HX), (f1, HC)):
-        remote(hid_ref, hbuf.at[f], HS, sems.at[sem], me, g).start()
+        remote(hbuf.at[f], hbuf.at[f], HS, sems.at[sem], me, g).start()
     for g in (f1, f2, f3):
         remote(gain_ref, gbuf.at[f], GS, sems.at[GR], me, g).start()
-    hbuf[f] = hid_ref[...]
     gbuf[f] = gain_ref[...]
 
     ids = ids_ref[...]
@@ -319,10 +328,10 @@
     def send_rows(g, m, kinds):
         column_ = near(g, m, 1)
         for off, member, slot_ in (
-            (0, i, 0),
+            (2, 1 - i, 3),
             (1, 0, 1 + i),
             (3, 1, 1 + i),
-            (2, 1 - i, 3),
+            (0, i, 0),
         )[kinds]:
             pair = lax.rem(zp + off, 4)
             remote(
@@ -341,7 +350,7 @@
 
         if 0 in steps[g]:
             lax.fori_loop(0, 2, one, 0)
-            each(g, 2, slice(1, 4))
+            each(g, 2, slice(0, 3))
             each(g, 3, slice(0, 4))
         else:
             lax.fori_loop(0, 4, one, 0)
@@ -350,13 +359,12 @@
     own_d.start()
     send_group(0, send_rows)
     send_group(1, send_rows)
+    send_group(2, send_rows)
+    send_group(3, send_rows)
     for g in range(4):
         span = pl.ds(16 * g, 16)
         wait(drecv.at[1, span], d_sem.at[g])
         remote(drecv.at[1, span], drecv.at[0, span], FS, fwd_sem.at[g], nb, f).start()
-        if g < 2:
-            wait(drecv.at[1, pl.ds(0, 16)], ds_sem.at[g])
-            send_group(g + 2, send_rows)
 
     wait(wg.at[early], sems.at[UX])
     remote(wu.at[shard(f2, 0, 176)], wu.at[shard(f2, 0, 176)], UFS, sems.at[UF], me, f1).start()
@@ -368,14 +376,14 @@
 
     def hidden(part_, kind, first_slot, rows, mine_buf):
         def widen(b, carry):
-            rows32[pl.ds(pl.multiple_of(384 * b, 384), 384), :] = (
+            wide32[pl.ds(pl.multiple_of(384 * b, 384), 384), :] = (
                 drecv[kind, pl.ds(pl.multiple_of(first_slot + 8 * b, 8), 8)].reshape(384, 128).astype(F32)
             )
             return carry
 
         lax.fori_loop(0, rows // 24, widen, 0)
         for c in range(16):
-            xbuf[0:rows, 128 * c : 128 * (c + 1)] = rows32[pl.ds(c, rows, stride=16), :].astype(BF16)
+            xbuf[0:rows, 128 * c : 128 * (c + 1)] = wide32[pl.ds(c, rows, stride=16), :].astype(BF16)
         x = xbuf[0:rows, :]
         for lo, hi in ((0, 256), (256, 512), (512, 704)):
             gate = lax.dot_general(x, wg[lo:hi, :], NT, preferred_element_type=F32)
@@ -397,38 +405,20 @@
             for c in range(4):
                 out32[pl.ds(4 * g + c, rows, stride=16), :] = out[:, 128 * c : 128 * (c + 1)]
 
-    def partner(first_group):
-        for g in range(2):
-            span = pl.ds(16 * (first_group + g), 16)
-            psend[span] = part32[768 * g : 768 * (g + 1), :].astype(BF16).reshape(16, 48, 128)
-            remote(psend.at[span], precv.at[span], PS, p_sem.at[first_group + g], nb, f).start()
-
-    part_b, part_c = abuf_b.at[0], abuf_b.at[1]
-    hidden(0, 1, 0, 192, abuf_a)
-    for g in range(2):
-        wait(drecv.at[0, pl.ds(0, 16)], fwd_sem.at[g])
-    hidden(1, 0, 0, 96, part_b)
-    share_on(0, abuf_a)
-    share_on(1, part_b)
-    for g in range(2, 4):
-        wait(drecv.at[0, pl.ds(0, 16)], fwd_sem.at[g])
-    hidden(2, 0, 32, 96, part_c)
-    lower(1, part_b, 96, part32)
-    partner(0)
-    lower(0, abuf_a, 192, rows32)
-    share_on(2, part_c)
-    lower(2, part_c, 96, part32)
-    partner(2)
+    def partner(g):
+        span = pl.ds(16 * g, 16)
+        psend[span] = part32[...].astype(BF16).reshape(16, 48, 128)
+        remote(psend.at[span], precv.at[span], PS, p_sem.at[g], nb, f).start()
 
     def send_back(g, m, kinds):
         column_ = near(g, m, -1)
         side = 2 * lax.rem(zp + 3 + 2 * i, 4)
-        for slot_, z in ((0, mz), (1, side), (2, side + 1), (3, 2 * lax.rem(zp + 2, 4) + 1 - i))[kinds]:
+        for slot_, z in ((3, 2 * lax.rem(zp + 2, 4) + 1 - i), (1, side), (2, side + 1), (0, mz))[kinds]:
             remote(
                 rsend.at[16 * g + 4 * m + slot_], rrecv.at[me // 2], RS, sems.at[RR], column_ + z, f
             ).start()
 
-    for g in range(4):
+    def give_back(g):
         span = pl.ds(16 * g, 16)
         wait(precv.at[span], p_sem.at[g])
         own = rows32[768 * g : 768 * (g + 1), :].astype(BF16).astype(F32)
@@ -438,6 +428,27 @@
             own_r = pltpu.make_async_copy(rsend.at[OWN], rrecv.at[me // 2], sems.at[RR])
             own_r.start()
         send_group(g, send_back)
+
+    parts = [abuf_b.at[g] for g in range(4)]
+    hidden(0, 1, 0, 192, abuf_a)
+    for g in range(4):
+        wait(drecv.at[0, pl.ds(0, 16)], fwd_sem.at[g])
+        if g > 0:
+            share_on(g, parts[g - 1])
+        hidden(g + 1, 0, 16 * g, 48, parts[g])
+        if g == 0:
+            share_on(0, abuf_a)
+        else:
+            lower(g, parts[g - 1], 48, part32)
+            partner(g - 1)
+        if g == 1:
+            lower(0, abuf_a, 192, rows32)
+    give_back(0)
+    share_on(4, parts[3])
+    lower(4, parts[3], 48, part32)
+    partner(3)
+    for g in range(1, 4):
+        give_back(g)
     wait(rrecv, sems.at[RR])
 
     def widen_back(b, carry):
@@ -455,7 +466,7 @@
         cols = slice(256 * s, 256 * (s + 1))
         mine_o = obuf[2 * f + s]
         att_ref[:, cols] = mine_o
-        summed = hid_ref[:, cols].astype(F32) + mine_o.astype(F32)
+        summed = hbuf[f, :, cols].astype(F32) + mine_o.astype(F32)
         mix_ref[:, cols] = (summed + total[:, cols]).astype(BF16)
 
     wait(qsend, sems.at[QS])
@@ -468,6 +479,8 @@
     wait(gbuf.at[pl.ds(0, 3)], sems.at[GS])
     wait(obuf.at[pl.ds(0, 4)], sems.at[OS])
     wait(obuf.at[pl.ds(0, 3)], sems.at[OFS])
+    wait(rrecv.at[pl.ds(0, 16)], ds_sem.at[0])
+    wait(rrecv.at[pl.ds(0, 16)], ds_sem.at[1])
     wait(rrecv.at[pl.ds(0, 15)], ds_sem.at[2])
     wait(rrecv.at[pl.ds(0, 16)], ds_sem.at[3])
     wait(drecv.at[0], sems.at[FS])
@@ -479,8 +492,8 @@
         wait(wg.at[early], sems.at[s])
     for s in range(3):
         wait(abuf_a.at[0], sems.at[AS + s])
-        wait(abuf_b.at[0, 0], sems.at[AS + 3 + s])
-        wait(abuf_b.at[0, 0], sems.at[AS + 6 + s])
+        for part_ in range(1, 5):
+            wait(abuf_b.at[0, 0], sems.at[AS + 3 * part_ + s])
 
 
 def per_device(
@@ -498,7 +511,6 @@
     lowering_matrix,
 ):
     src = (chosen_tile_lists[:, :, None] * 4 + jnp.arange(4, dtype=jnp.int32)).reshape(1, 1024)
-    gain = jnp.broadcast_to(premix_rmsnorm_scaling[None, :], (8, 512))
     vmem = pl.BlockSpec(memory_space=pltpu.VMEM)
     hbm = pl.BlockSpec(memory_space=pl.ANY)
     scratch = [
@@ -507,10 +519,11 @@
         pltpu.VMEM((16, 4, 2, 32, 128), BF16),
         pltpu.VMEM((16, 8, 32, 128), BF16),
         pltpu.VMEM((8, 16, 32, 128), BF16),
+        pltpu.VMEM((256, 512), BF16),
         pltpu.VMEM((2, 256, 256), BF16),
         pltpu.VMEM((256, 256), BF16),
         pltpu.VMEM((4, 256, 512), BF16),
-        pltpu.VMEM((4, 8, 512), F32),
+        pltpu.VMEM((4, 1, 512), F32),
         pltpu.VMEM((8, 256, 256), BF16),
         pltpu.VMEM((2, 256, 256), BF16),
         pltpu.VMEM((2, 2, 256, 128), F32),
@@ -519,12 +532,13 @@
         pltpu.VMEM((256, 768), BF16),
         pltpu.VMEM((256, 768), BF16),
         pltpu.VMEM((3072, 128), F32),
-        pltpu.VMEM((1536, 128), F32),
+        pltpu.VMEM((768, 128), F32),
+        pltpu.VMEM((3072, 128), F32),
         pltpu.VMEM((64, 48, 128), BF16),
         pltpu.VMEM((2, 64, 48, 128), BF16),
         pltpu.VMEM((192, 2048), BF16),
         pltpu.VMEM((4, 192, 704), BF16),
-        pltpu.VMEM((2, 4, 96, 704), BF16),
+        pltpu.VMEM((4, 4, 48, 704), BF16),
         pltpu.VMEM((64, 48, 128), BF16),
         pltpu.VMEM((64, 48, 128), BF16),
         pltpu.VMEM((64, 48, 128), BF16),
@@ -533,20 +547,21 @@
         pltpu.VMEM((704, 2048), BF16),
         pltpu.VMEM((704, 2048), BF16),
         pltpu.VMEM((704, 512), BF16),
-        pltpu.SemaphoreType.DMA((50,)),
+        pltpu.SemaphoreType.DMA((56,)),
         pltpu.SemaphoreType.DMA((4,)),
         pltpu.SemaphoreType.DMA((4,)),
         pltpu.SemaphoreType.DMA((4,)),
         pltpu.SemaphoreType.DMA((4,)),
         pltpu.SemaphoreType.DMA((4,)),
         pltpu.SemaphoreType.DMA((4,)),
-        pltpu.SemaphoreType.DMA((3, 3)),
+        pltpu.SemaphoreType.DMA((5, 3)),
+        pltpu.SemaphoreType.DMA((2,)),
     ]
     shape = jax.ShapeDtypeStruct((256, 512), BF16)
     return pl.pallas_call(
         layer_kernel,
         out_shape=(shape, shape),
-        in_specs=[pl.BlockSpec(memory_space=pltpu.SMEM)] + [vmem] * 8 + [hbm] * 3,
+        in_specs=[pl.BlockSpec(memory_space=pltpu.SMEM)] + [hbm] * 2 + [vmem] * 6 + [hbm] * 3,
         out_specs=(vmem, vmem),
         scratch_shapes=scratch,
         name="layer",
@@ -561,7 +576,7 @@
         memory_lookup_vectors.reshape(256, 512),
         content_vectors.reshape(256, 512),
         src,
-        gain,
+        premix_rmsnorm_scaling[None, :],
         routing_choice_ids.T,
         routing_shares.T,
         gating_matrix,

time: 166 us -> 163 us (0.982)
  Pallas kernels: 160 us -> 158 us
    pallas_call x1, Pallas kernels: 160 us -> 158 us  [per_device(): pl.pallas_call(layer_kernel, out_shape=(shape, shape), in_specs=[pl.Block...]
where the time goes in v4:
time: 163 us
  Pallas kernels  158 us (97%)
  local copies, waits for them, and re-layouts  3.58 us (2%)
    pallas_call x1, Pallas kernels, per_device(): pl.pallas_call(layer_kernel, out_shape=(shape, shape), in_specs=[pl.Block...  158 us

profile of v4, /device:TPU:1, one launch (start us, length us, event | category | flops | bytes accessed | tf_op | source)
XLA Modules:
  0.0 162.8 jit_solution(3026039385109726888)
XLA Ops:
  0.6 0.0 copy-start.6
  0.6 0.7 broadcast_multiply_fusion
  1.4 0.1 copy.15
  1.5 0.1 iota_add_fusion
  1.6 0.2 add.26.src_ref
  1.8 0.0 copy-done.6
  1.8 0.0 copy-start.7
  1.8 0.0 copy-start.2
  1.8 0.0 copy-start.3
  1.8 0.0 copy-start.4
  1.8 0.0 copy-start.5
  1.8 0.1 reshape.35.k_ref
  1.9 0.8 copy-done.7
  2.7 0.0 copy-start
  2.7 0.0 copy-start.1
  2.7 0.1 reshape.36.v_ref
  2.8 0.0 copy-done.2
  2.8 0.0 copy-done.3
  2.8 0.0 copy-done.4
  2.8 0.0 copy-done.5
  2.8 0.8 copy-done
  3.7 0.1 copy-done.1
  3.8 157.7 %layer.1 = (bf16[256,512]{1,0:T(8,128)(2,1)S(1)}, bf16[256,512]{1,0:T(8,128)(2,1)S(1)}) custom-call(f32[4]{0:T(128)S(1)} %copy-done.5, bf16[256,512]{1,0:T(8,128)(2,1)S(1)} %copy-done, bf16[256,512]{1,0:T(8,128)(2,1)S(1)} %copy-done.1, bf16[256,512]{1,0:T(8,128)(2,1)S(1)} %reshape.35.k_ref, bf16[256,512]{1,0:T(8,128)(2,1)S(1)} %reshape.36.v_ref, ...), custom_call_target="tpu_custom_call" | custom-call | flops 5000000000 | bytes 20000000 | tf_op jit(solution)/shard_map/layer/pallas_call | solution.py:561
  161.4 0.7 copy.18
  162.1 0.7 copy.19
Async XLA Ops:
  0.6 1.1 copy-start.6
  1.8 1.0 copy-start.7
  1.8 1.0 copy-start.2
  1.8 1.0 copy-start.3
  1.8 1.0 copy-start.4
  1.8 1.0 copy-start.5
  2.7 0.9 copy-start
  2.7 1.0 copy-start.1

commit v5 on v4

--- a/solution.py
+++ b/solution.py
@@ -109,11 +109,17 @@
 
     bar = pltpu.get_barrier_semaphore()
 
+    def hail(k, offs):
+        for off in offs:
+            to = lax.rem(xy + k, 16) * 8 + lax.rem(mz + 8 + off, 8)
+            pl.semaphore_signal(bar, inc=1, device_id=(to, f), device_id_type=MESH)
+
     def greet(k, carry):
-        pl.semaphore_signal(bar, inc=1, device_id=(lax.rem(me + k, N), f), device_id_type=MESH)
+        hail(k, (0, 2, -2, 2 * i - 1, 6 * i - 3))
         return carry
 
-    lax.fori_loop(1, N, greet, 0)
+    hail(0, (1, 2, 3, 4, 5, 6, 7))
+    lax.fori_loop(1, 16, greet, 0)
     for g in (f1, f2, f3):
         pl.semaphore_signal(bar, inc=1, device_id=(me, g), device_id_type=MESH)
         pl.semaphore_signal(bar, inc=1, device_id=(nb, g), device_id_type=MESH)
@@ -129,7 +135,7 @@
             got = jnp.dot(pick, v_ref[:, cols], preferred_element_type=F32).astype(BF16)
             kvs[:, :, half, head, 16:32, :] = got.reshape(16, 4, 16, 128)
 
-    pl.semaphore_wait(bar, N - 1 + 6)
+    pl.semaphore_wait(bar, 7 + 15 * 5 + 6)
 
     def remote(src, dst, s, r, ctx, ex):
         left = sems.at[s] if isinstance(s, int) else s

time: 163 us -> 163 us (level); the launches traced: 163 us -> 161 us
  Pallas kernels: 158 us -> 155 us
    pallas_call x1, Pallas kernels: 158 us -> 155 us  [per_device(): pl.pallas_call(layer_kernel, out_shape=(shape, shape), in_specs=[pl.Block...]
where the time goes in v5:
time: 163 us; the launch traced here: 161 us
  Pallas kernels  155 us (95%)
  local copies, waits for them, and re-layouts  3.58 us (2%)
    pallas_call x1, Pallas kernels, per_device(): pl.pallas_call(layer_kernel, out_shape=(shape, shape), in_specs=[pl.Block...  155 us

profile of v5, /device:TPU:1, one launch (start us, length us, event | category | flops | bytes accessed | tf_op | source)
XLA Modules:
  0.0 160.6 jit_solution(5637271958173934038)
XLA Ops:
  0.6 0.0 copy-start.6
  0.6 0.7 broadcast_multiply_fusion
  1.4 0.1 copy.15
  1.5 0.1 iota_add_fusion
  1.6 0.2 add.26.src_ref
  1.8 0.0 copy-done.6
  1.8 0.0 copy-start.7
  1.8 0.0 copy-start.2
  1.8 0.0 copy-start.3
  1.8 0.0 copy-start.4
  1.8 0.0 copy-start.5
  1.8 0.1 reshape.35.k_ref
  1.9 0.8 copy-done.7
  2.7 0.0 copy-start
  2.7 0.0 copy-start.1
  2.7 0.1 reshape.36.v_ref
  2.8 0.0 copy-done.2
  2.8 0.0 copy-done.3
  2.8 0.0 copy-done.4
  2.8 0.0 copy-done.5
  2.8 0.8 copy-done
  3.7 0.1 copy-done.1
  3.8 155.5 %layer.1 = (bf16[256,512]{1,0:T(8,128)(2,1)S(1)}, bf16[256,512]{1,0:T(8,128)(2,1)S(1)}) custom-call(f32[4]{0:T(128)S(1)} %copy-done.5, bf16[256,512]{1,0:T(8,128)(2,1)S(1)} %copy-done, bf16[256,512]{1,0:T(8,128)(2,1)S(1)} %copy-done.1, bf16[256,512]{1,0:T(8,128)(2,1)S(1)} %reshape.35.k_ref, bf16[256,512]{1,0:T(8,128)(2,1)S(1)} %reshape.36.v_ref, ...), custom_call_target="tpu_custom_call" | custom-call | flops 5000000000 | bytes 20000000 | tf_op jit(solution)/shard_map/layer/pallas_call | solution.py:567
  159.2 0.7 copy.18
  159.9 0.7 copy.19
Async XLA Ops:
  0.6 1.1 copy-start.6
  1.8 1.0 copy-start.7
  1.8 1.0 copy-start.2
  1.8 1.0 copy-start.3
  1.8 1.0 copy-start.4
  1.8 1.0 copy-start.5
  2.7 0.9 copy-start
  2.7 1.0 copy-start.1
